TPU v7x, 256 devices: a whole 4x4x8 slice. The times are simulated.
256 devices in a mesh: dp: 8 (over y, core), expert: 32 (over x, z).
Axes of the slice: x: 4, y: 4, z: 8, core: 2. Of those that a mesh axis runs over, the one named last changes fastest.
Arguments:
- tokens: bfloat16 [32768, 4096], P(('dp', 'expert')), may hold values from -6 to 6
- cotangent: bfloat16 [32768, 4096], P(('dp', 'expert')), may hold values from -1.5 to 1.5
- picks: int32 [8, 32, 64], P('dp'), may hold values from 0 to 4095, as said below
- gate_values: bfloat16 [8, 32, 64], P('dp', 'expert'), may hold values from 0.099609375 to 1
- w_gate: bfloat16 [32, 4096, 1536], P('expert', None, 'dp'), may hold values from -0.09375 to 0.09375
- w_up: bfloat16 [32, 4096, 1536], P('expert', None, 'dp'), may hold values from -0.09375 to 0.09375
- w_down: bfloat16 [32, 1536, 4096], P('expert', 'dp'), may hold values from -0.15625 to 0.15625
Outputs:
- d_tokens: bfloat16 [32768, 4096], P(('dp', 'expert'))
- d_gate_values: float32 [8, 32, 64], P('dp', 'expert')
- d_w_gate: bfloat16 [32, 4096, 1536], P('expert', None, 'dp')
- d_w_up: bfloat16 [32, 4096, 1536], P('expert', None, 'dp')
- d_w_down: bfloat16 [32, 1536, 4096], P('expert', 'dp')
Inputs may be any that keep to these rules, and one draw needn't show every extreme that they name: For each group and expert the 64 positions are distinct. Among the 128 tokens of any one device of a group, one expert picks at most 4, and in every group each expert picks exactly 4 from some device.
All inputs are finite; a program needn't handle non-finite values.
Results may differ from a plain program's by a relative error of at most 0.0057.
Values may be sent and summed in bfloat16 or wider, within the bound.
A program may use at most 128 MiB of HBM per device.

v0:
```python
import jax
import jax.numpy as jnp
from jax import lax
from jax.sharding import PartitionSpec as P


def on_device(tokens, cotangent, picks, gate_values, w_gate, w_up, w_down):
    tok_rows, width = tokens.shape
    shards = lax.axis_size("expert")
    own_index = lax.axis_index("expert")
    lists = picks[0]
    capacity = lists.shape[1]
    most = 2 * (capacity // shards)
    source = lists // tok_rows
    local = lists % tok_rows
    same = source[:, :, None] == source[:, None, :]
    before = jnp.arange(capacity)[None, :] < jnp.arange(capacity)[:, None]
    rank = jnp.sum((same & before[None, :, :]).astype(jnp.int32), axis=-1)
    mine = source == own_index
    slot_hot = (mine[:, None, :] & (rank[:, None, :] == jnp.arange(most)[None, :, None])).astype(
        jnp.int32
    )
    slot_index = jnp.sum(slot_hot * local[:, None, :], axis=-1)
    slot_valid = jnp.sum(slot_hot, axis=-1) > 0
    keep = slot_valid[:, :, None]
    send_rows = jnp.where(keep, tokens[slot_index], jnp.zeros((), jnp.bfloat16))
    send_dy = jnp.where(keep, cotangent[slot_index], jnp.zeros((), jnp.bfloat16))
    recv_rows, recv_dy = (
        lax.all_to_all(send_rows, "expert", split_axis=0, concat_axis=0, tiled=True),
        lax.all_to_all(send_dy, "expert", split_axis=0, concat_axis=0, tiled=True),
    )
    my_source = lax.dynamic_index_in_dim(source, own_index, 0, keepdims=False)
    my_rank = lax.dynamic_index_in_dim(rank, own_index, 0, keepdims=False)
    flat = my_source * most + my_rank
    rows = recv_rows.reshape(shards * most, width)[flat]
    dyr = recv_dy.reshape(shards * most, width)[flat]
    all_rows, all_dy, all_gv = (
        lax.all_gather(rows, "dp", axis=0, tiled=True),
        lax.all_gather(dyr, "dp", axis=0, tiled=True),
        lax.all_gather(gate_values[0, 0], "dp", axis=0, tiled=True),
    )
    w_g = w_gate[0]
    w_u = w_up[0]
    w_d = w_down[0]
    gate = jnp.dot(all_rows, w_g, preferred_element_type=jnp.float32)
    up = jnp.dot(all_rows, w_u, preferred_element_type=jnp.float32)
    act = jax.nn.silu(gate)
    hidden = (act * up).astype(jnp.bfloat16)
    back = lax.dot_general(
        all_dy, w_d, (((1,), (1,)), ((), ())), preferred_element_type=jnp.float32
    )
    out_part = jnp.dot(hidden, w_d, preferred_element_type=jnp.float32)
    out_mine = lax.psum_scatter(out_part, "dp", scatter_dimension=0, tiled=True)
    score = jnp.sum(out_mine * dyr.astype(jnp.float32), axis=-1)
    gv = all_gv.astype(jnp.float32)
    d_hidden = gv[:, None] * back
    sig = jax.nn.sigmoid(gate)
    d_gate = (d_hidden * up * sig * (1.0 + gate * (1.0 - sig))).astype(jnp.bfloat16)
    d_up = (d_hidden * act).astype(jnp.bfloat16)
    d_out = (gv[:, None] * all_dy.astype(jnp.float32)).astype(jnp.bfloat16)
    contract_rows = (((0,), (0,)), ((), ()))
    dwd = lax.dot_general(hidden, d_out, contract_rows, preferred_element_type=jnp.float32).astype(
        jnp.bfloat16
    )
    dwg = lax.dot_general(
        all_rows, d_gate, contract_rows, preferred_element_type=jnp.float32
    ).astype(jnp.bfloat16)
    dwu = lax.dot_general(all_rows, d_up, contract_rows, preferred_element_type=jnp.float32).astype(
        jnp.bfloat16
    )
    contract_hidden = (((1,), (1,)), ((), ()))
    total = lax.dot_general(d_gate, w_g, contract_hidden, preferred_element_type=jnp.float32)
    d_pick = lax.psum_scatter(
        total + lax.dot_general(d_up, w_u, contract_hidden, preferred_element_type=jnp.float32),
        "dp",
        scatter_dimension=0,
        tiled=True,
    ).astype(jnp.bfloat16)
    back_slots = jnp.zeros((shards * most, width), jnp.bfloat16).at[flat].set(d_pick)
    returned = lax.all_to_all(
        back_slots.reshape(shards, most, width), "expert", split_axis=0, concat_axis=0, tiled=True
    )
    token_hot = slot_valid[None, :, :] & (
        slot_index[None, :, :] == jnp.arange(tok_rows)[:, None, None]
    )
    token_hot = token_hot.reshape(tok_rows, shards * most).astype(jnp.bfloat16)
    d_tokens = jnp.dot(
        token_hot, returned.reshape(shards * most, width), preferred_element_type=jnp.float32
    )
    return (
        d_tokens.astype(jnp.bfloat16),
        score.reshape(1, 1, capacity),
        dwg[None],
        dwu[None],
        dwd[None],
    )


def solution(mesh):
    in_specs = (
        P(("dp", "expert"), None),
        P(("dp", "expert"), None),
        P("dp", None, None),
        P("dp", "expert", None),
        P("expert", None, "dp"),
        P("expert", None, "dp"),
        P("expert", "dp", None),
    )
    out_specs = (
        P(("dp", "expert"), None),
        P("dp", "expert", None),
        P("expert", None, "dp"),
        P("expert", None, "dp"),
        P("expert", "dp", None),
    )
    return jax.shard_map(
        on_device, mesh=mesh, in_specs=in_specs, out_specs=out_specs, check_vma=False
    )
```

profile of v0, /device:TPU:1, one launch (start us, length us, event | category | flops | bytes accessed | tf_op | source)
XLA Modules:
  0.0 270.5 jit_solution(13848955566813531945)
XLA Ops:
  10.3 4.6 %gather_fusion.2 = bf16[128,4096]{1,0:T(8,128)(2,1)} fusion(bf16[128,4096]{1,0:T(8,128)(2,1)} %param.7, s32[1024]{0:T(1024)S(1)} %pad_clamp_fusion.1), kind=kCustom, calls=%fused_computation.2 | custom fusion | bytes 2097664 | tf_op jit(solution)/shard_map/gather | solution.py:26
  14.9 2.2 reshape.198
  17.2 2.2 gather_fusion
  20.8 3.5 %broadcast_select_fusion.1 = (bf16[32,4,4096]{2,1,0:T(4,128)(2,1)}, bf16[32,4,4096]{2,1,0:T(4,128)(2,1)}) fusion(bf16[32,4,4096]{2,1,0:T(4,128)(2,1)S(1)} %reshape.182, pred[32,4]{1,0:T(8,128)(4,1)S(1)} %copy.20, bf16[32,4,4096]{2,1,0:T(4,128)(2,1)} %reshape.198), kind=kLoop, calls=%fused_computation.32 | loop fusion | flops 1048576 | bytes 4194432 | tf_op jit(solution)/shard_map/jit(_where)/select_n | solution.py:27
  24.3 12.0 %all-to-all-start.1 = ((bf16[32,4,4096]{2,1,0:T(4,128)(2,1)}), bf16[32,4,4096]{2,1,0:T(4,128)(2,1)}, u32[]{:S(2)}, u32[]{:S(2)}) async-start(bf16[32,4,4096]{2,1,0:T(4,128)(2,1)} %get-tuple-element.13), calls=%async_computation.1 | async-start | bytes 2097152 | tf_op jit(solution)/shard_map/all_to_all | solution.py:29
  36.4 24.5 %all-to-all-done.1 = bf16[32,4,4096]{2,1,0:T(4,128)(2,1)} async-done(((bf16[32,4,4096]{2,1,0:T(4,128)(2,1)}), bf16[32,4,4096]{2,1,0:T(4,128)(2,1)}, u32[]{:S(2)}, u32[]{:S(2)}) %all-to-all-start.1) | async-done | bytes 1048608 | tf_op jit(solution)/shard_map/all_to_all | solution.py:29
  64.0 33.5 %all_to_all.15 = bf16[32,4,4096]{2,1,0:T(4,128)(2,1)} all-to-all(bf16[32,4,4096]{2,1,0:T(4,128)(2,1)} %get-tuple-element.12), channel_id=1, replica_groups=mesh['dp'=8,'expert'=32] {'expert'}, dimensions={0} | all-to-all | bytes 2097152 | tf_op jit(solution)/shard_map/all_to_all | solution.py:30
  98.8 1.7 gather_fusion.1
  102.1 17.1 %all-reduce = bf16[512]{0:T(512)(128)(2,1)S(1)} all-reduce(bf16[512]{0:T(512)(128)(2,1)S(1)} %dynamic-update-slice), channel_id=2, replica_groups=mesh['dp'=8,'expert'=32] {'dp'}, use_global_device_ids=true, to_apply=%add | all-reduce | flops 512 | bytes 2048
  119.3 5.0 %fusion.7 = f32[512,192]{0,1:T(8,128)} fusion(bf16[512,4096]{1,0:T(8,128)(2,1)} %all-gather.8.cloned.1.call-done, bf16[1,4096,192]{1,2,0:T(8,128)(2,1)} %param.11), kind=kOutput, calls=%fused_computation.18 | convolution fusion | flops 805306368 | bytes 6160384 | tf_op jit(solution)/shard_map/dot_general | solution.py:45
  124.3 12.5 %all-gather.6.cloned.1.call-done = bf16[512,4096]{1,0:T(8,128)(2,1)} async-done(((bf16[64,4096]{1,0:T(8,128)(2,1)}), bf16[512,4096]{1,0:T(8,128)(2,1)}) %all-gather.6.cloned.1.call-update) | async-done | bytes 4194320 | tf_op jit(solution)/shard_map/all_gather | solution.py:39
  136.8 3.9 %fusion.16 = f32[512,192]{0,1:T(8,128)S(1)} fusion(bf16[512,4096]{1,0:T(8,128)(2,1)} %all-gather.6.cloned.1.call-done, bf16[1,192,4096]{2,1,0:T(8,128)(2,1)S(1)} %copy-done.6, f32[512]{0:T(512)S(1)} %convert_element_type.58), kind=kOutput, calls=%fused_computation.27 | convolution fusion | flops 805404672 | bytes 6162432 | tf_op jit(solution)/shard_map/dot_general | solution.py:49
  140.7 2.4 multiply_convert_fusion.2
  144.5 4.5 %convolution_add_fusion = f32[512,4096]{1,0:T(8,128)} fusion(f32[512,4096]{1,0:T(8,128)S(1)} %fusion.5, bf16[512,192]{0,1:T(8,128)(2,1)S(1)} %get-tuple-element.11, bf16[1,4096,192]{1,2,0:T(8,128)(2,1)S(1)} %copy-done), kind=kOutput, calls=%fused_computation.6 | convolution fusion | flops 807403520 | bytes 18546688 | tf_op jit(solution)/shard_map/dot_general | solution.py:74
  149.1 5.4 %fusion.12 = f32[512,4096]{1,0:T(8,128)} fusion(bf16[512,192]{0,1:T(8,128)(2,1)} %get-tuple-element.9, bf16[1,192,4096]{2,1,0:T(8,128)(2,1)S(1)} %copy-done.6), kind=kOutput, calls=%fused_computation.23 | convolution fusion | flops 805306368 | bytes 10158080 | tf_op jit(solution)/shard_map/dot_general | solution.py:52
  154.5 48.6 %reduce-scatter.3.cloned.1.call-done = f32[64,4096]{1,0:T(8,128)} async-done(((f32[512,4096]{1,0:T(8,128)}), f32[64,4096]{1,0:T(8,128)}) %reduce-scatter.3.cloned.1.call-update) | async-done | bytes 1048592 | tf_op jit(solution)/shard_map/reduce_scatter | solution.py:73
  203.1 2.4 scatter_custom_fusion
  206.7 9.7 %all-to-all-start.2 = ((bf16[32,4,4096]{2,1,0:T(4,128)(2,1)}), bf16[32,4,4096]{2,1,0:T(4,128)(2,1)S(1)}, u32[]{:S(2)}, u32[]{:S(2)}) async-start(bf16[32,4,4096]{2,1,0:T(4,128)(2,1)} %reshape.179), calls=%async_computation.3 | async-start | bytes 2097152 | tf_op jit(solution)/shard_map/all_to_all | solution.py:80
  216.4 5.1 %fusion.2 = bf16[1,4096,192]{1,2,0:T(8,128)(2,1)} fusion(bf16[512,192]{0,1:T(8,128)(2,1)S(1)} %get-tuple-element.10, bf16[512,4096]{1,0:T(8,128)(2,1)} %all-gather.8.cloned.1.call-done), kind=kOutput, calls=%fused_computation.13 | convolution fusion | flops 806092800 | bytes 5963776 | tf_op jit(solution)/shard_map/dot_general | solution.py:65
  221.5 2.1 fusion.3
  224.5 2.3 fusion.1
  226.8 33.4 %reduce-scatter.5.cloned.1.call-done = f32[64,4096]{1,0:T(8,128)} async-done(((f32[512,4096]{1,0:T(8,128)}), f32[64,4096]{1,0:T(8,128)}) %reduce-scatter.5.cloned.1.call-update) | async-done | bytes 1048592 | tf_op jit(solution)/shard_map/reduce_scatter | solution.py:53
  260.2 1.9 multiply_reduce_fusion
  262.1 1.9 fusion
  (57 shorter events, 13.4 us)
Async XLA Ops:
  7.2 133.5 %copy-start = (bf16[1,4096,192]{1,2,0:T(8,128)(2,1)S(1)}, bf16[1,4096,192]{1,2,0:T(8,128)(2,1)}, u32[]{:S(2)}) copy-start(bf16[1,4096,192]{1,2,0:T(8,128)(2,1)} %param.12) | copy-start | bytes 4718596
  10.3 6.9 %copy-start.1 = (bf16[128,4096]{1,0:T(8,128)(2,1)S(1)}, bf16[128,4096]{1,0:T(8,128)(2,1)}, u32[]{:S(2)}) copy-start(bf16[128,4096]{1,0:T(8,128)(2,1)} %param.8) | copy-start | bytes 3145732
  24.3 36.6 %all-to-all-start.1 = ((bf16[32,4,4096]{2,1,0:T(4,128)(2,1)}), bf16[32,4,4096]{2,1,0:T(4,128)(2,1)}, u32[]{:S(2)}, u32[]{:S(2)}) async-start(bf16[32,4,4096]{2,1,0:T(4,128)(2,1)} %get-tuple-element.13), calls=%async_computation.1 | async-start | bytes 2097152 | tf_op jit(solution)/shard_map/all_to_all | solution.py:29
  36.3 83.0 %all-gather.8.cloned.1.call-start = ((), (), s32[]{:S(2)}) async-start(), calls=%async_computation.8 | async-start | bytes 4718592 | tf_op jit(solution)/shard_map/all_gather | solution.py:38
  63.9 72.9 %all-gather.6.cloned.1.call-start = ((), (), s32[]{:S(2)}) async-start(), calls=%async_computation.7 | async-start | bytes 4718592 | tf_op jit(solution)/shard_map/all_gather | solution.py:39
  97.5 3.1 %copy-start.10 = (u32[256]{0:T(256)S(1)}, u32[256]{0:T(256)}, u32[]{:S(2)}) copy-start(u32[256]{0:T(256)} %constant.65) | copy-start | bytes 3076
  97.5 4.4 %copy-start.9 = (bf16[1,1,64]{2,1,0:T(2,128)(2,1)S(1)}, bf16[1,1,64]{2,1,0:T(2,128)(2,1)}, u32[]{:S(2)}) copy-start(bf16[1,1,64]{2,1,0:T(2,128)(2,1)} %param.10) | copy-start | bytes 388
  100.5 36.3 %copy-start.6 = (bf16[1,192,4096]{2,1,0:T(8,128)(2,1)S(1)}, bf16[1,192,4096]{2,1,0:T(8,128)(2,1)}, u32[]{:S(2)}) copy-start(bf16[1,192,4096]{2,1,0:T(8,128)(2,1)} %param.13) | copy-start | bytes 4718596
  100.5 102.6 %reduce-scatter.3.cloned.1.call-start = ((), (), s32[]{:S(2)}) async-start(), calls=%async_computation.5 | async-start | bytes 9437184 | tf_op jit(solution)/shard_map/reduce_scatter | solution.py:73
  136.8 3.9 %copy-start.2 = (bf16[512,4096]{1,0:T(8,128)(2,1)S(1)}, bf16[512,4096]{1,0:T(8,128)(2,1)}, u32[]{:S(2)}) copy-start(bf16[512,4096]{1,0:T(8,128)(2,1)} %all-gather.8.cloned.1.call-done) | copy-start | bytes 12582916
  136.8 3.9 %copy-start.11 = (f32[512,192]{0,1:T(8,128)S(1)}, f32[512,192]{0,1:T(8,128)}, u32[]{:S(2)}) copy-start(f32[512,192]{0,1:T(8,128)} %fusion.7) | copy-start | bytes 1179652
  140.7 2.4 copy-start.5
  149.0 111.1 %reduce-scatter.5.cloned.1.call-start = ((), (), s32[]{:S(2)}) async-start(), calls=%async_computation.6 | async-start | bytes 9437184 | tf_op jit(solution)/shard_map/reduce_scatter | solution.py:53
  206.7 55.4 %all-to-all-start.2 = ((bf16[32,4,4096]{2,1,0:T(4,128)(2,1)}), bf16[32,4,4096]{2,1,0:T(4,128)(2,1)S(1)}, u32[]{:S(2)}, u32[]{:S(2)}) async-start(bf16[32,4,4096]{2,1,0:T(4,128)(2,1)} %reshape.179), calls=%async_computation.3 | async-start | bytes 2097152 | tf_op jit(solution)/shard_map/all_to_all | solution.py:80
  216.4 5.1 %copy-start.3 = (bf16[512,4096]{1,0:T(8,128)(2,1)S(1)}, bf16[512,4096]{1,0:T(8,128)(2,1)}, u32[]{:S(2)}) copy-start(bf16[512,4096]{1,0:T(8,128)(2,1)} %all-gather.8.cloned.1.call-done) | copy-start | bytes 12582916
  221.5 2.1 copy-start.7
  221.5 3.0 %copy-start.8 = (bf16[512,4096]{1,0:T(8,128)(2,1)S(1)}, bf16[512,4096]{1,0:T(8,128)(2,1)}, u32[]{:S(2)}) copy-start(bf16[512,4096]{1,0:T(8,128)(2,1)} %all-gather.6.cloned.1.call-done) | copy-start | bytes 12582916
  224.5 35.7 %copy-start.4 = (bf16[64,4096]{1,0:T(8,128)(2,1)S(1)}, bf16[64,4096]{1,0:T(8,128)(2,1)}, u32[]{:S(2)}) copy-start(bf16[64,4096]{1,0:T(8,128)(2,1)} %gather_fusion.1) | copy-start | bytes 1572868
Sparse Core Ops, SparseCore 0:
  64.1 36.1 all-gather.7
  102.1 34.6 all-gather.5
  149.1 53.9 reduce-scatter.2
  205.5 54.5 reduce-scatter.4
where the time goes:
time: 271 us
  waiting for transfers between devices  119 us (44%)
  blocking collectives  50.6 us (19%)
  matrix products  34 us (13%)
  starting transfers between devices  21.9 us (8%)
  local copies, waits for them, and re-layouts  19.8 us (7%)
  between operations  14.6 us (5%)
  other arithmetic  10.6 us (4%)
    reduce_scatter x1, waiting for transfers between devices, on_device(): lax.psum_scatter(total + lax.dot_general(d_up, w_u, contract_hidden, pref...  48.6 us
    all_to_all x1, blocking collectives, on_device(): lax.all_to_all(send_dy, 'expert', split_axis=0, concat_axis=0, tiled=True)  33.5 us
    reduce_scatter x1, waiting for transfers between devices, on_device(): out_mine = lax.psum_scatter(out_part, 'dp', scatter_dimension=0, tiled=True)  33.4 us
    all_to_all x1, waiting for transfers between devices, on_device(): lax.all_to_all(send_rows, 'expert', split_axis=0, concat_axis=0, tiled=True)  24.5 us
    unnamed x1, blocking collectives  17.1 us
    all_gather x1, waiting for transfers between devices, on_device(): lax.all_gather(dyr, 'dp', axis=0, tiled=True)  12.5 us
    all_to_all x1, starting transfers between devices, on_device(): lax.all_to_all(send_rows, 'expert', split_axis=0, concat_axis=0, tiled=True)  12 us
    all_to_all x1, starting transfers between devices, on_device(): lax.all_to_all(back_slots.reshape(shards, most, width), 'expert', split_a...  9.74 us
  transfers between devices with their start and end apart: 6, of which 4 were waited for; matrix products, arithmetic and copies ran while one was open for 11% of the time, Pallas kernels for 0%

commit v1 on v0

--- a/solution.py
+++ b/solution.py
@@ -49,9 +49,8 @@
     back = lax.dot_general(
         all_dy, w_d, (((1,), (1,)), ((), ())), preferred_element_type=jnp.float32
     )
-    out_part = jnp.dot(hidden, w_d, preferred_element_type=jnp.float32)
-    out_mine = lax.psum_scatter(out_part, "dp", scatter_dimension=0, tiled=True)
-    score = jnp.sum(out_mine * dyr.astype(jnp.float32), axis=-1)
+    score_part = jnp.sum(hidden.astype(jnp.float32) * back, axis=-1)
+    score = lax.psum_scatter(score_part, "dp", scatter_dimension=0, tiled=True)
     gv = all_gv.astype(jnp.float32)
     d_hidden = gv[:, None] * back
     sig = jax.nn.sigmoid(gate)
@@ -71,7 +70,9 @@
     contract_hidden = (((1,), (1,)), ((), ()))
     total = lax.dot_general(d_gate, w_g, contract_hidden, preferred_element_type=jnp.float32)
     d_pick = lax.psum_scatter(
-        total + lax.dot_general(d_up, w_u, contract_hidden, preferred_element_type=jnp.float32),
+        (
+            total + lax.dot_general(d_up, w_u, contract_hidden, preferred_element_type=jnp.float32)
+        ).astype(jnp.bfloat16),
         "dp",
         scatter_dimension=0,
         tiled=True,

time: 271 us -> 235 us (0.87)
  waiting for transfers between devices: 119 us -> 72.7 us
  blocking collectives: 50.6 us -> 66.6 us
  matrix products: 34 us -> 27.7 us
  other arithmetic: 10.6 us -> 6.31 us
    reduce_scatter x2 -> x1, waiting for transfers between devices: 81.9 us -> 37.1 us  [on_device(): lax.psum_scatter((total + lax.dot_general(d_up, w_u, contract_hidden, pre...]
    unnamed x1 -> x2, blocking collectives: 17.1 us -> 33.1 us
    dot_general x1 -> x0, matrix products: 5.45 us -> none  [on_device(): out_part = jnp.dot(hidden, w_d, preferred_element_type=jnp.float32)]
  transfers between devices with their start and end apart: 6 -> 5, of which waited for: 4 -> 3; matrix products, arithmetic and copies ran while one was open for 11% -> 9% of each run, Pallas kernels for 0% -> 0%
where the time goes in v1:
time: 235 us; the launch traced here: 232 us
  waiting for transfers between devices  72.7 us (31%)
  blocking collectives  66.6 us (28%)
  matrix products  27.7 us (12%)
  local copies, waits for them, and re-layouts  22.3 us (9%)
  starting transfers between devices  21.6 us (9%)
  between operations  15.3 us (7%)
  other arithmetic  6.31 us (3%)
    reduce_scatter x1, waiting for transfers between devices, on_device(): lax.psum_scatter((total + lax.dot_general(d_up, w_u, contract_hidden, pre...  37.1 us
    all_to_all x1, blocking collectives, on_device(): lax.all_to_all(send_dy, 'expert', split_axis=0, concat_axis=0, tiled=True)  33.5 us
    unnamed x2, blocking collectives  33.1 us
    all_to_all x1, waiting for transfers between devices, on_device(): lax.all_to_all(send_rows, 'expert', split_axis=0, concat_axis=0, tiled=True)  24.5 us
    all_to_all x1, starting transfers between devices, on_device(): lax.all_to_all(send_rows, 'expert', split_axis=0, concat_axis=0, tiled=True)  12 us
    all_gather x1, waiting for transfers between devices, on_device(): lax.all_gather(dyr, 'dp', axis=0, tiled=True)  11 us
    all_to_all x1, starting transfers between devices, on_device(): lax.all_to_all(back_slots.reshape(shards, most, width), 'expert', split_a...  9.53 us
    gather x2, local copies, waits for them, and re-layouts, on_device(): send_rows = jnp.where(keep, tokens[slot_index], jnp.zeros((), jnp.bfloat16))  6.86 us
  transfers between devices with their start and end apart: 5, of which 3 were waited for; matrix products, arithmetic and copies ran while one was open for 9% of the time, Pallas kernels for 0%

profile of v1, /device:TPU:1, one launch (start us, length us, event | category | flops | bytes accessed | tf_op | source)
XLA Modules:
  0.0 232.5 jit_solution(646568483426997327)
XLA Ops:
  10.3 4.6 %gather_fusion.2 = bf16[128,4096]{1,0:T(8,128)(2,1)} fusion(bf16[128,4096]{1,0:T(8,128)(2,1)} %param.7, s32[1024]{0:T(1024)S(1)} %pad_clamp_fusion.1), kind=kCustom, calls=%fused_computation.2 | custom fusion | bytes 2097664 | tf_op jit(solution)/shard_map/gather | solution.py:26
  14.9 2.2 reshape.198
  17.2 2.2 gather_fusion
  19.3 1.5 reshape.182
  20.8 3.5 %broadcast_select_fusion.1 = (bf16[32,4,4096]{2,1,0:T(4,128)(2,1)}, bf16[32,4,4096]{2,1,0:T(4,128)(2,1)}) fusion(bf16[32,4,4096]{2,1,0:T(4,128)(2,1)S(1)} %reshape.182, pred[32,4]{1,0:T(8,128)(4,1)S(1)} %copy.20, bf16[32,4,4096]{2,1,0:T(4,128)(2,1)} %reshape.198), kind=kLoop, calls=%fused_computation.28 | loop fusion | flops 1048576 | bytes 4194432 | tf_op jit(solution)/shard_map/jit(_where)/select_n | solution.py:27
  24.3 12.0 %all-to-all-start.1 = ((bf16[32,4,4096]{2,1,0:T(4,128)(2,1)}), bf16[32,4,4096]{2,1,0:T(4,128)(2,1)}, u32[]{:S(2)}, u32[]{:S(2)}) async-start(bf16[32,4,4096]{2,1,0:T(4,128)(2,1)} %get-tuple-element.14), calls=%async_computation.1 | async-start | bytes 2097152 | tf_op jit(solution)/shard_map/all_to_all | solution.py:29
  36.4 24.5 %all-to-all-done.1 = bf16[32,4,4096]{2,1,0:T(4,128)(2,1)} async-done(((bf16[32,4,4096]{2,1,0:T(4,128)(2,1)}), bf16[32,4,4096]{2,1,0:T(4,128)(2,1)}, u32[]{:S(2)}, u32[]{:S(2)}) %all-to-all-start.1) | async-done | bytes 1048608 | tf_op jit(solution)/shard_map/all_to_all | solution.py:29
  62.2 1.7 gather_fusion.3
  64.0 33.5 %all_to_all.15 = bf16[32,4,4096]{2,1,0:T(4,128)(2,1)} all-to-all(bf16[32,4,4096]{2,1,0:T(4,128)(2,1)} %get-tuple-element.13), channel_id=1, replica_groups=mesh['dp'=8,'expert'=32] {'expert'}, dimensions={0} | all-to-all | bytes 2097152 | tf_op jit(solution)/shard_map/all_to_all | solution.py:30
  98.8 1.7 gather_fusion.1
  102.1 17.1 %all-reduce = bf16[512]{0:T(512)(128)(2,1)S(1)} all-reduce(bf16[512]{0:T(512)(128)(2,1)S(1)} %dynamic-update-slice), channel_id=2, replica_groups=mesh['dp'=8,'expert'=32] {'dp'}, use_global_device_ids=true, to_apply=%add | all-reduce | flops 512 | bytes 2048
  119.3 4.7 %fusion.7 = f32[512,192]{0,1:T(8,128)} fusion(bf16[512,4096]{1,0:T(8,128)(2,1)} %all-gather.8.cloned.1.call-done, bf16[1,4096,192]{1,2,0:T(8,128)(2,1)S(1)} %copy-done), kind=kOutput, calls=%fused_computation.18 | convolution fusion | flops 805306368 | bytes 6160384 | tf_op jit(solution)/shard_map/dot_general | solution.py:45
  124.0 2.4 %fusion.10 = f32[512,192]{0,1:T(8,128)} fusion(bf16[512,4096]{1,0:T(8,128)(2,1)S(1)} %copy-done.2, bf16[1,4096,192]{1,2,0:T(8,128)(2,1)S(1)} %copy-done.4), kind=kOutput, calls=%fused_computation.21 | convolution fusion | flops 805306368 | bytes 6160384 | tf_op jit(solution)/shard_map/dot_general | solution.py:46
  126.4 11.0 %all-gather.6.cloned.1.call-done = bf16[512,4096]{1,0:T(8,128)(2,1)} async-done(((bf16[64,4096]{1,0:T(8,128)(2,1)}), bf16[512,4096]{1,0:T(8,128)(2,1)}) %all-gather.6.cloned.1.call-update) | async-done | bytes 4194320 | tf_op jit(solution)/shard_map/all_gather | solution.py:39
  137.4 5.2 %multiply_reduce_fusion = (f32[512]{0:T(512)S(1)}, bf16[512,192]{0,1:T(8,128)(2,1)}, bf16[512,192]{0,1:T(8,128)(2,1)S(1)}, bf16[512,192]{0,1:T(8,128)(2,1)S(1)}) fusion(f32[512,192]{0,1:T(8,128)} %fusion.10, f32[512,192]{0,1:T(8,128)} %fusion.7, f32[512]{0:T(512)S(1)} %convert_element_type.58, bf16[512,4096]{1,0:T(8,128)(2,1)} %all-gather.6.cloned.1.call-done, ...), kind=kOutput, calls=%fused_computation.31 | convolution fusion | flops 807173632 | bytes 7147520 | tf_op jit(solution)/shard_map/dot_general | solution.py:49
  143.8 3.3 %add_convert_fusion = bf16[512,4096]{1,0:T(8,128)(2,1)} fusion(f32[512,4096]{1,0:T(8,128)S(1)} %fusion.5, bf16[512,192]{0,1:T(8,128)(2,1)S(1)} %get-tuple-element.12, bf16[1,4096,192]{1,2,0:T(8,128)(2,1)S(1)} %copy-done.4), kind=kOutput, calls=%fused_computation.6 | convolution fusion | flops 809500672 | bytes 14352384 | tf_op jit(solution)/shard_map/dot_general | solution.py:74
  147.2 37.1 %reduce-scatter.2.cloned.1.call-done = bf16[64,4096]{1,0:T(8,128)(2,1)} async-done(((bf16[512,4096]{1,0:T(8,128)(2,1)}), bf16[64,4096]{1,0:T(8,128)(2,1)}) %reduce-scatter.2.cloned.1.call-update) | async-done | bytes 524304 | tf_op jit(solution)/shard_map/reduce_scatter | solution.py:72
  184.3 2.2 scatter_custom_fusion
  187.6 9.5 %all-to-all-start.2 = ((bf16[32,4,4096]{2,1,0:T(4,128)(2,1)}), bf16[32,4,4096]{2,1,0:T(4,128)(2,1)S(1)}, u32[]{:S(2)}, u32[]{:S(2)}) async-start(bf16[32,4,4096]{2,1,0:T(4,128)(2,1)} %reshape.179), calls=%async_computation.3 | async-start | bytes 2097152 | tf_op jit(solution)/shard_map/all_to_all | solution.py:81
  197.8 16.0 %all-reduce.1 = f32[512]{0:T(512)S(1)} all-reduce(f32[512]{0:T(512)S(1)} %get-tuple-element.7), channel_id=6, replica_groups=mesh['dp'=8,'expert'=32] {'dp'}, use_global_device_ids=true, to_apply=%region_6.7.clone | all-reduce | flops 512 | bytes 4096
  214.4 4.6 %fusion.2 = bf16[1,4096,192]{1,2,0:T(8,128)(2,1)} fusion(bf16[512,192]{0,1:T(8,128)(2,1)S(1)} %get-tuple-element.11, bf16[512,4096]{1,0:T(8,128)(2,1)} %all-gather.8.cloned.1.call-done), kind=kOutput, calls=%fused_computation.13 | convolution fusion | flops 806092800 | bytes 5963776 | tf_op jit(solution)/shard_map/dot_general | solution.py:64
  219.0 2.1 fusion.3
  221.8 2.3 fusion.1
  224.1 1.9 fusion
  (50 shorter events, 10.6 us)
Async XLA Ops:
  7.2 112.1 %copy-start = (bf16[1,4096,192]{1,2,0:T(8,128)(2,1)S(1)}, bf16[1,4096,192]{1,2,0:T(8,128)(2,1)}, u32[]{:S(2)}) copy-start(bf16[1,4096,192]{1,2,0:T(8,128)(2,1)} %param.11) | copy-start | bytes 4718596
  10.3 6.9 %copy-start.1 = (bf16[128,4096]{1,0:T(8,128)(2,1)S(1)}, bf16[128,4096]{1,0:T(8,128)(2,1)}, u32[]{:S(2)}) copy-start(bf16[128,4096]{1,0:T(8,128)(2,1)} %param.8) | copy-start | bytes 3145732
  24.3 36.6 %all-to-all-start.1 = ((bf16[32,4,4096]{2,1,0:T(4,128)(2,1)}), bf16[32,4,4096]{2,1,0:T(4,128)(2,1)}, u32[]{:S(2)}, u32[]{:S(2)}) async-start(bf16[32,4,4096]{2,1,0:T(4,128)(2,1)} %get-tuple-element.14), calls=%async_computation.1 | async-start | bytes 2097152 | tf_op jit(solution)/shard_map/all_to_all | solution.py:29
  36.3 82.9 %all-gather.8.cloned.1.call-start = ((), (), s32[]{:S(2)}) async-start(), calls=%async_computation.6 | async-start | bytes 4718592 | tf_op jit(solution)/shard_map/all_gather | solution.py:38
  36.4 61.1 %copy-start.5 = (s32[64]{0:T(128)}, s32[64]{0:T(128)S(1)}, u32[]{:S(2)}) copy-start(s32[64]{0:T(128)S(1)} %fusion.26) | copy-start | bytes 772
  63.9 73.5 %all-gather.6.cloned.1.call-start = ((), (), s32[]{:S(2)}) async-start(), calls=%async_computation.5 | async-start | bytes 4718592 | tf_op jit(solution)/shard_map/all_gather | solution.py:39
  97.5 3.1 %copy-start.6 = (u32[256]{0:T(256)S(1)}, u32[256]{0:T(256)}, u32[]{:S(2)}) copy-start(u32[256]{0:T(256)} %constant.65) | copy-start | bytes 3076
  97.5 4.4 %copy-start.8 = (bf16[1,1,64]{2,1,0:T(2,128)(2,1)S(1)}, bf16[1,1,64]{2,1,0:T(2,128)(2,1)}, u32[]{:S(2)}) copy-start(bf16[1,1,64]{2,1,0:T(2,128)(2,1)} %param.10) | copy-start | bytes 388
  100.5 23.5 %copy-start.4 = (bf16[1,4096,192]{1,2,0:T(8,128)(2,1)S(1)}, bf16[1,4096,192]{1,2,0:T(8,128)(2,1)}, u32[]{:S(2)}) copy-start(bf16[1,4096,192]{1,2,0:T(8,128)(2,1)} %param.12) | copy-start | bytes 4718596
  100.5 83.7 %reduce-scatter.2.cloned.1.call-start = ((), (), s32[]{:S(2)}) async-start(), calls=%async_computation.4 | async-start | bytes 4718592 | tf_op jit(solution)/shard_map/reduce_scatter | solution.py:72
  119.3 4.7 %copy-start.2 = (bf16[512,4096]{1,0:T(8,128)(2,1)S(1)}, bf16[512,4096]{1,0:T(8,128)(2,1)}, u32[]{:S(2)}) copy-start(bf16[512,4096]{1,0:T(8,128)(2,1)} %all-gather.8.cloned.1.call-done) | copy-start | bytes 12582916
  187.6 36.4 %all-to-all-start.2 = ((bf16[32,4,4096]{2,1,0:T(4,128)(2,1)}), bf16[32,4,4096]{2,1,0:T(4,128)(2,1)S(1)}, u32[]{:S(2)}, u32[]{:S(2)}) async-start(bf16[32,4,4096]{2,1,0:T(4,128)(2,1)} %reshape.179), calls=%async_computation.3 | async-start | bytes 2097152 | tf_op jit(solution)/shard_map/all_to_all | solution.py:81
  213.8 5.2 %copy-start.3 = (bf16[512,4096]{1,0:T(8,128)(2,1)S(1)}, bf16[512,4096]{1,0:T(8,128)(2,1)}, u32[]{:S(2)}) copy-start(bf16[512,4096]{1,0:T(8,128)(2,1)} %all-gather.8.cloned.1.call-done) | copy-start | bytes 12582916
  219.0 2.8 %copy-start.7 = (bf16[512,4096]{1,0:T(8,128)(2,1)S(1)}, bf16[512,4096]{1,0:T(8,128)(2,1)}, u32[]{:S(2)}) copy-start(bf16[512,4096]{1,0:T(8,128)(2,1)} %all-gather.6.cloned.1.call-done) | copy-start | bytes 12582916
  219.0 2.8 %copy-start.9 = (bf16[512,192]{0,1:T(8,128)(2,1)S(1)}, bf16[512,192]{0,1:T(8,128)(2,1)}, u32[]{:S(2)}) copy-start(bf16[512,192]{0,1:T(8,128)(2,1)} %get-tuple-element.8) | copy-start | bytes 589828
Sparse Core Ops, SparseCore 0:
  64.1 36.1 all-gather.7
  102.7 34.6 all-gather.5
  147.3 36.9 reduce-scatter.1

commit v2 on v0

v2 whole, which is shorter than its diff:
```python
import functools

import jax
import jax.numpy as jnp
from jax import lax
from jax.experimental import pallas as pl
from jax.experimental.pallas import tpu as pltpu
from jax.sharding import PartitionSpec as P

MESH = pl.DeviceIdType.MESH
BF = jnp.bfloat16
F32 = jnp.float32
NT = (((1,), (1,)), ((), ()))
SLOTS = 4
SUB = 4
ROWS = SLOTS * SUB
CH = 2
RC = 2


def dot(a, b):
    return jnp.dot(a, b, preferred_element_type=F32)


def dot_nt(a, b):
    return lax.dot_general(a, b, NT, preferred_element_type=F32)


def al(i, m):
    return pl.multiple_of(i, m)


def kernel(
    experts, tok, cot, picks, gates, wg_h, wu_h, wd_h,
    dtok, score, dwg_h, dwu_h, dwd_h,
    sendb, recvb, alls, gvb, gv_all, wg, wu, wd, wsib, gate, up, back, dgu, dgs, tr,
    a_s, a_r, b_s, b_r, dg_own, dg_x, ret_s, ret_r, sc_p, sc_r, dwg, dwu, dwd,
    d_send, d_recv, g_send, g_recv, small_s, small_r, sib_s, sib_r, rs_s, rs_r, r_send, r_recv, loc,
):
    tok_rows, width = tok.shape
    cap = gvb.shape[0]
    dp = lax.axis_index("dp")
    ex = lax.axis_index("expert")
    y = dp // 2
    k = lax.rem(dp, 2)
    y_up, y_dn, y_op = lax.rem(y + 1, 4), lax.rem(y + 3, 4), lax.rem(y + 2, 4)
    up_d, dn_d, op_d, sib = y_up * 2 + k, y_dn * 2 + k, y_op * 2 + k, y * 2 + 1 - k
    half = width // 2
    cw = width // CH
    sw = cw // SUB
    nrow = experts * ROWS

    loads = [
        pltpu.make_async_copy(h.at[0], v, loc.at[i])
        for i, (h, v) in enumerate(((wg_h, wg), (wu_h, wu), (wd_h, wd)))
    ]
    for c in loads:
        c.start()

    pending = []
    barrier = pltpu.get_barrier_semaphore()

    def hail(d, carry):
        pl.semaphore_signal(
            barrier, inc=1, device_id=(dp, lax.rem(ex + d, experts)), device_id_type=MESH
        )
        return carry

    def hail_dp(d, carry):
        pl.semaphore_signal(
            barrier, inc=1, device_id=(lax.rem(dp + d, 8), ex), device_id_type=MESH
        )
        return carry

    lax.fori_loop(1, experts, hail, 0)
    lax.fori_loop(1, 8, hail_dp, 0)

    def copy(src, dst, s, r, to):
        return pltpu.make_async_remote_copy(
            src_ref=src, dst_ref=dst, send_sem=s, recv_sem=r, device_id=(to, ex), device_id_type=MESH
        )

    def push(src, dst, s, r, to):
        d = copy(src, dst, s, r, to)
        d.start()
        pending.append(d.wait_send)
        return d

    def spread(src, dst, s, r):
        def send(d, carry):
            to = lax.rem(ex + d, experts)
            pltpu.make_async_remote_copy(
                src_ref=src.at[pl.ds(al(to * ROWS, ROWS), ROWS)],
                dst_ref=dst.at[pl.ds(al(ex * ROWS, ROWS), ROWS)],
                send_sem=s, recv_sem=r, device_id=(dp, to), device_id_type=MESH,
            ).start()
            return carry

        lax.fori_loop(1, experts, send, 0)
        pending.append(lambda: await_bytes(src, s))

    def await_bytes(ref, sem):
        part = ref.at[pl.ds(0, nrow - ROWS)]
        pltpu.make_async_copy(part, part, sem).wait()

    shift = tok_rows.bit_length() - 1
    lists = picks[0]
    mine_f = jnp.where((lists >> shift) == ex, 1.0, 0.0)
    ahead = lax.broadcasted_iota(jnp.int32, (cap, cap), 0) < lax.broadcasted_iota(jnp.int32, (cap, cap), 1)
    place = dot(mine_f.astype(BF), jnp.where(ahead, 1.0, 0.0).astype(BF))
    token = ((lists & (tok_rows - 1)) + 1).astype(F32) * mine_f
    lane = lax.broadcasted_iota(jnp.int32, (experts, 128), 1)
    slots = jnp.zeros((experts, 128), F32)
    for s in range(SLOTS):
        at = jnp.sum(jnp.where(place == s, token, 0.0), axis=-1, keepdims=True)
        slots = jnp.where(lane == s, at, slots)
    grow = lax.broadcasted_iota(jnp.int32, (nrow, experts), 0) // ROWS
    spot = jnp.where(grow == lax.broadcasted_iota(jnp.int32, (nrow, experts), 1), 1.0, 0.0)
    spread_slots = dot(spot.astype(BF), slots.astype(BF))
    pick_lane = lax.rem(lax.broadcasted_iota(jnp.int32, (nrow, 128), 0), SLOTS)
    at_lane = lax.broadcasted_iota(jnp.int32, (nrow, 128), 1)
    sidx_c = jnp.sum(jnp.where(at_lane == pick_lane, spread_slots, 0.0), axis=-1, keepdims=True) - 1.0

    row_sub = lax.rem(lax.broadcasted_iota(jnp.int32, (nrow, tok_rows), 0) // SLOTS, SUB)
    col_tok = lax.broadcasted_iota(jnp.int32, (nrow, tok_rows), 1)
    match = sidx_c == col_tok.astype(F32)
    hots = [jnp.where(match & (row_sub == b), 1.0, 0.0).astype(BF) for b in range(SUB)]
    own = pl.ds(al(ex * ROWS, ROWS), ROWS)
    for q in range(2 * CH):
        src = tok if q < CH else cot
        base = (q % CH) * cw
        acc = dot(hots[0], src[:, base : base + sw])
        for b in range(1, SUB):
            acc += dot(hots[b], src[:, base + b * sw : base + (b + 1) * sw])
        sendb[q] = acc.astype(BF)
        recvb[q, own, :] = sendb[q, own, :]
        if q == 0:
            pl.semaphore_wait(barrier, experts - 1 + 7)
        spread(sendb.at[q], recvb.at[q], d_send.at[q], d_recv.at[q])

    own_row = picks[0, pl.ds(ex, 1), :]
    src_row = jnp.broadcast_to((own_row >> shift).astype(F32), (128, cap))
    src_col = src_row.T
    behind = lax.broadcasted_iota(jnp.int32, (cap, cap), 0) > lax.broadcasted_iota(jnp.int32, (cap, cap), 1)
    twins = jnp.where((src_col[:, :cap] == src_row[:cap]) & behind, 1.0, 0.0)
    rfl_c = src_col[:, 0:1] * ROWS + jnp.sum(twins, axis=-1, keepdims=True)
    rfl_r = jnp.broadcast_to(rfl_c, (cap, 128)).T[0:1]
    sidx_r = jnp.broadcast_to(sidx_c, (nrow, 128)).T[0:1]
    gvb[...] = jnp.broadcast_to(gates[0].astype(F32), (128, cap)).T

    mine = pl.ds(al(dp * cap, cap), cap)
    gv_all[mine, :] = gvb[...]

    def send_gv(d, carry):
        copy(gvb, gv_all.at[mine], small_s.at[0], small_r.at[0], lax.rem(dp + d, 8)).start()
        return carry

    lax.fori_loop(1, 8, send_gv, 0)
    gv_part = gv_all.at[pl.ds(0, 7 * cap)]
    pending.append(pltpu.make_async_copy(gv_part, gv_part, small_s.at[0]).wait)
    other = pl.ds(al((1 - k) * half, half), half)
    ws0 = push(wg_h.at[0, :, other], wsib.at[0], sib_s.at[0], sib_r.at[0], sib)
    ws1 = push(wu_h.at[0, :, other], wsib.at[1], sib_s.at[1], sib_r.at[1], sib)
    for c in loads:
        c.wait()

    lane_row = lax.broadcasted_iota(jnp.int32, (cap, nrow), 1).astype(F32)
    for q in range(2 * CH):
        a, c = q // CH, q % CH
        cols = pl.ds(c * cw, cw)

        def blk(i, lo=0, n=cap):
            return alls.at[a, pl.ds(al(i * cap + lo, 16), n), cols]

        def pass_on(j, i, to, lo=0, n=cap):
            return push(blk(i, lo, n), blk(i, lo, n), g_send.at[q, j], g_recv.at[q, j], to)

        await_bytes(recvb.at[q], d_recv.at[q])
        for b in range(SUB):
            rhot = jnp.where(rfl_c + b * SLOTS == lane_row, 1.0, 0.0).astype(BF)
            alls[a, mine, c * cw + b * sw : c * cw + (b + 1) * sw] = dot(rhot, recvb[q]).astype(BF)
        hc = cap // 2
        c_up = pass_on(0, dp, up_d)
        c_dn = pass_on(1, dp, dn_d)
        s0 = pass_on(2, dp, sib)
        c_up.wait_recv()
        f_up = pass_on(3, dn_d, up_d, 0, hc)
        s1 = pass_on(4, dn_d, sib)
        c_dn.wait_recv()
        f_dn = pass_on(5, up_d, dn_d, hc, hc)
        s2 = pass_on(6, up_d, sib)
        f_up.wait_recv()
        s3 = pass_on(7, op_d, sib, 0, hc)
        f_dn.wait_recv()
        s4 = pass_on(8, op_d, sib, hc, hc)
        for s in (s0, s1, s2, s3, s4):
            s.wait_recv()

        kt = 512

        if a == 0:
            if c == 0:
                gate[...] = jnp.zeros_like(gate)
                up[...] = jnp.zeros_like(up)

            def fwd(i, carry):
                kk = pl.ds(al(c * cw + i * kt, kt), kt)
                r = alls[0, :, kk]
                gate[...] += dot_nt(r, wg[:, kk])
                up[...] += dot_nt(r, wu[:, kk])
                return carry

            lax.fori_loop(0, cw // kt, fwd, 0)
        else:
            if c == 0:
                back[...] = jnp.zeros_like(back)

            def bwd(i, carry):
                kk = pl.ds(al(c * cw + i * kt, kt), kt)
                back[...] += dot_nt(alls[1, :, kk], wd[:, kk])
                return carry

            lax.fori_loop(0, cw // kt, bwd, 0)

    pltpu.make_async_copy(gv_part, gv_part, small_r.at[0]).wait()

    def pointwise(i, carry):
        r = pl.ds(al(i * 128, 128), 128)
        g, u, bk = gate[r, :], up[r, :], back[r, :]
        gv = gv_all[r, 0:1]
        s = jax.nn.sigmoid(g)
        act = g * s
        hidden = (act * u).astype(BF).astype(F32)
        sc_p[r, :] = jnp.broadcast_to(jnp.sum(hidden * bk, axis=-1, keepdims=True), (128, 128))
        dh = gv * bk
        dgate = (dh * u * s * (1.0 + g * (1.0 - s))).astype(BF)
        dup = (dh * act).astype(BF)
        dgu[0, r, :] = dgate
        dgu[1, r, :] = dup
        tr[0, :, r] = hidden.T.astype(BF)
        tr[1, :, r] = dgate.astype(F32).T.astype(BF)
        tr[2, :, r] = dup.astype(F32).T.astype(BF)
        return carry

    lax.fori_loop(0, 4, pointwise, 0)
    dx = push(dgu, dgs, sib_s.at[2], sib_r.at[2], sib)

    def send_score(d, carry):
        to = lax.rem(dp + d, 8)
        copy(
            sc_p.at[pl.ds(al(to * cap, cap), cap)], sc_r.at[lax.rem(8 - d, 8)],
            small_s.at[1], small_r.at[1], to,
        ).start()
        return carry

    lax.fori_loop(1, 8, send_score, 0)
    sc_part = sc_r.at[pl.ds(1, 7)]
    pending.append(pltpu.make_async_copy(sc_part, sc_part, small_s.at[1]).wait)
    ws0.wait_recv()
    ws1.wait_recv()
    dx.wait_recv()

    two = 2 * cap
    fw = half // RC
    hw = fw // 2

    def part(yy, c):
        r = pl.ds(al(yy * two, two), two)
        w_at = pl.ds(al(k * half + c * fw, fw), fw)
        o_at = pl.ds(c * fw, fw)
        t = dot(dgu[0, r, :], wg[:, w_at])
        t += dot(dgu[1, r, :], wu[:, w_at])
        t += dot(dgs[0, r, :], wsib[0, :, o_at])
        t += dot(dgs[1, r, :], wsib[1, :, o_at])
        return t

    a_cp, b_cp, x_cp = [], [], []
    for c in range(RC):
        t = part(y_op, c)
        a_s[c, 0] = t[:, :hw].astype(BF)
        a_s[c, 1] = t[:, hw:].astype(BF)
        for j, to in ((0, up_d), (1, dn_d)):
            a_cp.append(push(a_s.at[c, j], a_r.at[c, j], rs_s.at[c, j], rs_r.at[c, j], to))
    for c in range(RC):
        for j, (yy, to) in enumerate(((y_up, up_d), (y_dn, dn_d))):
            t = part(yy, c)
            a_cp[2 * c + j].wait_recv()
            at = slice(0, hw) if j == 0 else slice(hw, fw)
            rest = slice(hw, fw) if j == 0 else slice(0, hw)
            b_s[c, j, :, at] = (t[:, at] + a_r[c, j].astype(F32)).astype(BF)
            b_s[c, j, :, rest] = t[:, rest].astype(BF)
            b_cp.append(
                push(b_s.at[c, j], b_r.at[c, j], rs_s.at[c, 2 + j], rs_r.at[c, 2 + j], to)
            )
    for c in range(RC):
        t = part(y, c)
        b_cp[2 * c].wait_recv()
        b_cp[2 * c + 1].wait_recv()
        t += b_r[c, 0].astype(F32) + b_r[c, 1].astype(F32)
        dg_own[c] = t.astype(BF)
        x_cp.append(
            push(
                dg_own.at[c, pl.ds(al((1 - k) * cap, cap), cap)], dg_x.at[c],
                rs_s.at[c, 4], rs_r.at[c, 4], sib,
            )
        )

    row_i = lax.broadcasted_iota(jnp.int32, (nrow, cap), 0).astype(F32)
    for c in range(RC):
        x_cp[c].wait_recv()
        mine_half = dg_own[c, pl.ds(al(k * cap, cap), cap), :]
        theirs = dg_x[c]
        first = k == 0
        h0 = jnp.where(first, mine_half, theirs)
        h1 = jnp.where(first, theirs, mine_half)
        acc = jnp.zeros((nrow, hw), F32)
        for b in range(SUB):
            hot = jnp.where(rfl_r + b * SLOTS == row_i, 1.0, 0.0).astype(BF)
            src = h0 if b < 2 else h1
            acc += dot(hot, src[:, (b % 2) * hw : (b % 2 + 1) * hw])
        ret_s[c] = acc.astype(BF)
        ret_r[c, own, :] = ret_s[c, own, :]
        spread(ret_s.at[c], ret_r.at[c], r_send.at[c], r_recv.at[c])

    nt = 512

    def grads(i, carry):
        cc = pl.ds(al(i * nt, nt), nt)
        dyt = alls[1, :, cc].astype(F32)
        d_out = (gv_all[:, 0:1] * dyt).astype(BF)
        dwd[:, cc] = dot(tr[0], d_out).astype(BF)
        r = alls[0, :, cc]
        dwg[:, cc] = dot(tr[1], r).astype(BF)
        dwu[:, cc] = dot(tr[2], r).astype(BF)
        return carry

    lax.fori_loop(0, width // nt, grads, 0)
    stores = [
        pltpu.make_async_copy(v, h.at[0], loc.at[i])
        for i, (h, v) in enumerate(((dwg_h, dwg), (dwu_h, dwu), (dwd_h, dwd)))
    ]
    for c in stores:
        c.start()
    pltpu.make_async_copy(sc_part, sc_part, small_r.at[1]).wait()
    total = sc_p[mine, :]
    for j in range(1, 8):
        total += sc_r[j]
    score[0] = total.T[0:1]

    sub_r = lax.rem(lax.broadcasted_iota(jnp.int32, (tok_rows, nrow), 1) // SLOTS, SUB)
    tok_i = lax.broadcasted_iota(jnp.int32, (tok_rows, nrow), 0).astype(F32)
    tmatch = sidx_r == tok_i
    for c in range(RC):
        await_bytes(ret_r.at[c], r_recv.at[c])
        for b in range(SUB):
            hot = jnp.where(tmatch & (sub_r == b), 1.0, 0.0).astype(BF)
            col = (b // 2) * half + c * fw + (b % 2) * hw
            dtok[:, col : col + hw] = dot(hot, ret_r[c]).astype(BF)

    for wait in pending:
        wait()
    for c in stores:
        c.wait()


def on_device(tokens, cotangent, picks, gate_values, w_gate, w_up, w_down):
    tok_rows, width = tokens.shape
    experts = lax.axis_size("expert")
    groups = lax.axis_size("dp")
    ff = w_down.shape[1]
    cap = picks.shape[2]
    nrow = experts * ROWS
    half = width // 2
    cw = width // CH
    fw = half // RC
    rows = groups * cap
    vm = pl.BlockSpec(memory_space=pltpu.VMEM)
    hbm = pl.BlockSpec(memory_space=pl.ANY)
    dma = pltpu.SemaphoreType.DMA
    d_tokens, score, dwg, dwu, dwd = pl.pallas_call(
        functools.partial(kernel, experts),
        out_shape=(
            jax.ShapeDtypeStruct((tok_rows, width), BF),
            jax.ShapeDtypeStruct((1, 1, cap), F32),
            jax.ShapeDtypeStruct((1, ff, width), BF),
            jax.ShapeDtypeStruct((1, ff, width), BF),
            jax.ShapeDtypeStruct(w_down.shape, BF),
        ),
        in_specs=[vm] * 4 + [hbm] * 3,
        out_specs=[vm] * 2 + [hbm] * 3,
        scratch_shapes=[
            pltpu.VMEM((2 * CH, nrow, cw // SUB), BF),
            pltpu.VMEM((2 * CH, nrow, cw // SUB), BF),
            pltpu.VMEM((2, rows, width), BF),
            pltpu.VMEM((cap, 128), F32),
            pltpu.VMEM((rows, 128), F32),
            pltpu.VMEM((ff, width), BF),
            pltpu.VMEM((ff, width), BF),
            pltpu.VMEM((ff, width), BF),
            pltpu.VMEM((2, ff, half), BF),
            pltpu.VMEM((rows, ff), F32),
            pltpu.VMEM((rows, ff), F32),
            pltpu.VMEM((rows, ff), F32),
            pltpu.VMEM((2, rows, ff), BF),
            pltpu.VMEM((2, rows, ff), BF),
            pltpu.VMEM((3, ff, rows), BF),
            pltpu.VMEM((RC, 2, 2 * cap, fw // 2), BF),
            pltpu.VMEM((RC, 2, 2 * cap, fw // 2), BF),
            pltpu.VMEM((RC, 2, 2 * cap, fw), BF),
            pltpu.VMEM((RC, 2, 2 * cap, fw), BF),
            pltpu.VMEM((RC, 2 * cap, fw), BF),
            pltpu.VMEM((RC, cap, fw), BF),
            pltpu.VMEM((RC, nrow, fw // 2), BF),
            pltpu.VMEM((RC, nrow, fw // 2), BF),
            pltpu.VMEM((rows, 128), F32),
            pltpu.VMEM((groups, cap, 128), F32),
            pltpu.VMEM((ff, width), BF),
            pltpu.VMEM((ff, width), BF),
            pltpu.VMEM((ff, width), BF),
            dma((2 * CH,)), dma((2 * CH,)),
            dma((2 * CH, 9)), dma((2 * CH, 9)),
            dma((2,)), dma((2,)),
            dma((3,)), dma((3,)),
            dma((RC, 5)), dma((RC, 5)),
            dma((RC,)), dma((RC,)),
            dma((3,)),
        ],
        compiler_params=pltpu.CompilerParams(
            collective_id=0, has_side_effects=True, vmem_limit_bytes=58 * 2**20
        ),
        cost_estimate=pl.CostEstimate(
            flops=2 * 8 * rows * width * ff, bytes_accessed=12 * 2**20, transcendentals=rows * ff
        ),
    )(
        tokens, cotangent, picks, gate_values,
        jnp.swapaxes(w_gate, 1, 2), jnp.swapaxes(w_up, 1, 2), w_down,
    )
    return d_tokens, score, jnp.swapaxes(dwg, 1, 2), jnp.swapaxes(dwu, 1, 2), dwd


def solution(mesh):
    in_specs = (
        P(("dp", "expert"), None),
        P(("dp", "expert"), None),
        P("dp", None, None),
        P("dp", "expert", None),
        P("expert", None, "dp"),
        P("expert", None, "dp"),
        P("expert", "dp", None),
    )
    out_specs = (
        P(("dp", "expert"), None),
        P("dp", "expert", None),
        P("expert", None, "dp"),
        P("expert", None, "dp"),
        P("expert", "dp", None),
    )
    return jax.shard_map(
        on_device, mesh=mesh, in_specs=in_specs, out_specs=out_specs, check_vma=False
    )
```

time: 271 us -> 152 us (0.56)
  Pallas kernels: 0 us -> 143 us
  waiting for transfers between devices: 119 us -> 0 us
  blocking collectives: 50.6 us -> 0 us
  matrix products: 34 us -> 0 us
  starting transfers between devices: 21.9 us -> 0 us
  between operations: 14.6 us -> 0.66 us
  local copies, waits for them, and re-layouts: 19.8 us -> 8.02 us
  other arithmetic: 10.6 us -> 0 us
    pallas_call x0 -> x1, Pallas kernels: none -> 143 us  [on_device(): pl.pallas_call(functools.partial(kernel, experts), out_shape=(jax.ShapeDt...]
    reduce_scatter x2 -> x0, waiting for transfers between devices: 81.9 us -> none  [the longest x1 48.6 us: on_device(): lax.psum_scatter(total + lax.dot_general(d_up, w_u, contract_hidden, pref...]
    dot_general x10 -> x0, matrix products: 34 us -> none  [the longest x1 5.45 us: on_device(): out_part = jnp.dot(hidden, w_d, preferred_element_type=jnp.float32)]
    all_to_all x1 -> x0, blocking collectives: 33.5 us -> none  [on_device(): lax.all_to_all(send_dy, 'expert', split_axis=0, concat_axis=0, tiled=True)]
    all_to_all x2 -> x0, waiting for transfers between devices: 24.5 us -> none  [the longest x1 24.5 us: on_device(): lax.all_to_all(send_rows, 'expert', split_axis=0, concat_axis=0, tiled=True)]
    all_to_all x2 -> x0, starting transfers between devices: 21.7 us -> none  [the longest x1 12 us: on_device(): lax.all_to_all(send_rows, 'expert', split_axis=0, concat_axis=0, tiled=True)]
    unnamed x1 -> x0, blocking collectives: 17.1 us -> none
    gather x6 -> x0, local copies, waits for them, and re-layouts: 13.8 us -> none  [the longest x2 6.86 us: on_device(): send_rows = jnp.where(keep, tokens[slot_index], jnp.zeros((), jnp.bfloat16))]
  transfers between devices with their start and end apart: 6 -> 0, of which waited for: 4 -> 0; matrix products, arithmetic and copies ran while one was open for 11% -> 0% of each run, Pallas kernels for 0% -> 0%
where the time goes in v2:
time: 152 us
  Pallas kernels  143 us (94%)
  local copies, waits for them, and re-layouts  8.02 us (5%)
    pallas_call x1, Pallas kernels, on_device(): pl.pallas_call(functools.partial(kernel, experts), out_shape=(jax.ShapeDt...  143 us
    unnamed x13, local copies, waits for them, and re-layouts  8.02 us

profile of v2, /device:TPU:1, one launch (start us, length us, event | category | flops | bytes accessed | tf_op | source)
XLA Modules:
  0.0 152.0 jit_solution(8012941837330611028)
XLA Ops:
  0.6 143.3 %shard_map.110 = (bf16[128,4096]{1,0:T(8,128)(2,1)}, f32[1,1,64]{2,1,0:T(1,128)}, bf16[1,192,4096]{2,1,0:T(8,128)(2,1)}, bf16[1,192,4096]{2,1,0:T(8,128)(2,1)}, bf16[1,192,4096]{2,1,0:T(8,128)(2,1)}) custom-call(bf16[128,4096]{1,0:T(8,128)(2,1)} %tok.1, bf16[128,4096]{1,0:T(8,128)(2,1)} %cot.1, s32[1,32,64]{2,1,0:T(8,128)} %picks.1, ...), custom_call_target="tpu_custom_call" | custom-call | flops 6442450944 | bytes 12582912 | tf_op jit(solution)/shard_map/pallas_call | solution.py:380
  143.9 0.0 copy-start.3
  143.9 0.0 copy-start.2
  143.9 2.4 %copy.17 = bf16[128,4096]{1,0:T(8,128)(2,1)} copy(bf16[128,4096]{1,0:T(8,128)(2,1)} %get-tuple-element.20) | data formatting | bytes 2097152
  146.3 0.0 copy-done.3
  146.3 0.5 copy.18
  146.9 0.0 copy-done.2
  146.9 0.0 copy-start.1
  146.9 1.1 copy.19
  148.0 0.8 copy-done.1
  148.8 0.0 copy-start
  148.8 1.1 copy.20
  150.0 0.8 copy-done
  150.8 1.1 copy.21
Async XLA Ops:
  143.9 2.4 %copy-start.3 = (f32[1,1,64]{2,1,0:T(1,128)S(1)}, f32[1,1,64]{2,1,0:T(1,128)}, u32[]{:S(2)}) copy-start(f32[1,1,64]{2,1,0:T(1,128)} %get-tuple-element.21) | copy-start | bytes 772
  143.9 2.9 %copy-start.2 = (bf16[1,192,4096]{2,1,0:T(8,128)(2,1)S(1)}, bf16[1,192,4096]{2,1,0:T(8,128)(2,1)}, u32[]{:S(2)}) copy-start(bf16[1,192,4096]{2,1,0:T(8,128)(2,1)} %get-tuple-element.12) | copy-start | bytes 4718596
  146.9 2.0 %copy-start.1 = (bf16[1,192,4096]{2,1,0:T(8,128)(2,1)S(1)}, bf16[1,192,4096]{2,1,0:T(8,128)(2,1)}, u32[]{:S(2)}) copy-start(bf16[1,192,4096]{2,1,0:T(8,128)(2,1)} %get-tuple-element.13) | copy-start | bytes 4718596
  148.8 2.0 %copy-start = (bf16[1,192,4096]{2,1,0:T(8,128)(2,1)S(1)}, bf16[1,192,4096]{2,1,0:T(8,128)(2,1)}, u32[]{:S(2)}) copy-start(bf16[1,192,4096]{2,1,0:T(8,128)(2,1)} %get-tuple-element.24) | copy-start | bytes 4718596

commit v3 on v2

--- a/solution.py
+++ b/solution.py
@@ -15,7 +15,9 @@
 SUB = 4
 ROWS = SLOTS * SUB
 CH = 2
-RC = 2
+RC = 4
+PIECE = 64
+DEPTH = 2
 
 
 def dot(a, b):
@@ -33,7 +35,7 @@
 def kernel(
     experts, tok, cot, picks, gates, wg_h, wu_h, wd_h,
     dtok, score, dwg_h, dwu_h, dwd_h,
-    sendb, recvb, alls, gvb, gv_all, wg, wu, wd, wsib, gate, up, back, dgu, dgs, tr,
+    sendb, recvb, alls, gvb, gv_all, wg, wu, wd, wsib, gate, up, back, hid, dgu, dgs, tr,
     a_s, a_r, b_s, b_r, dg_own, dg_x, ret_s, ret_r, sc_p, sc_r, dwg, dwu, dwd,
     d_send, d_recv, g_send, g_recv, small_s, small_r, sib_s, sib_r, rs_s, rs_r, r_send, r_recv, loc,
 ):
@@ -126,6 +128,10 @@
     match = sidx_c == col_tok.astype(F32)
     hots = [jnp.where(match & (row_sub == b), 1.0, 0.0).astype(BF) for b in range(SUB)]
     own = pl.ds(al(ex * ROWS, ROWS), ROWS)
+
+    def dispatch(q):
+        spread(sendb.at[q], recvb.at[q], d_send.at[q], d_recv.at[q])
+
     for q in range(2 * CH):
         src = tok if q < CH else cot
         base = (q % CH) * cw
@@ -136,7 +142,8 @@
         recvb[q, own, :] = sendb[q, own, :]
         if q == 0:
             pl.semaphore_wait(barrier, experts - 1 + 7)
-        spread(sendb.at[q], recvb.at[q], d_send.at[q], d_recv.at[q])
+        if q < DEPTH:
+            dispatch(q)
 
     own_row = picks[0, pl.ds(ex, 1), :]
     src_row = jnp.broadcast_to((own_row >> shift).astype(F32), (128, cap))
@@ -165,154 +172,148 @@
         c.wait()
 
     lane_row = lax.broadcasted_iota(jnp.int32, (cap, nrow), 1).astype(F32)
-    for q in range(2 * CH):
-        a, c = q // CH, q % CH
-        cols = pl.ds(c * cw, cw)
-
-        def blk(i, lo=0, n=cap):
-            return alls.at[a, pl.ds(al(i * cap + lo, 16), n), cols]
-
-        def pass_on(j, i, to, lo=0, n=cap):
-            return push(blk(i, lo, n), blk(i, lo, n), g_send.at[q, j], g_recv.at[q, j], to)
-
+    hc = cap // 2
+    kt = 512
+    hops = {}
+
+    def blk(q, i, lo, n):
+        return alls.at[q // CH, pl.ds(al(i * cap + lo, 16), n), pl.ds((q % CH) * cw, cw)]
+
+    def pass_on(q, j, i, to, lo=0, n=cap):
+        hops[q, j] = push(blk(q, i, lo, n), blk(q, i, lo, n), g_send.at[q, j], g_recv.at[q, j], to)
+
+    def arrive(q):
         await_bytes(recvb.at[q], d_recv.at[q])
         for b in range(SUB):
             rhot = jnp.where(rfl_c + b * SLOTS == lane_row, 1.0, 0.0).astype(BF)
-            alls[a, mine, c * cw + b * sw : c * cw + (b + 1) * sw] = dot(rhot, recvb[q]).astype(BF)
-        hc = cap // 2
-        c_up = pass_on(0, dp, up_d)
-        c_dn = pass_on(1, dp, dn_d)
-        s0 = pass_on(2, dp, sib)
-        c_up.wait_recv()
-        f_up = pass_on(3, dn_d, up_d, 0, hc)
-        s1 = pass_on(4, dn_d, sib)
-        c_dn.wait_recv()
-        f_dn = pass_on(5, up_d, dn_d, hc, hc)
-        s2 = pass_on(6, up_d, sib)
-        f_up.wait_recv()
-        s3 = pass_on(7, op_d, sib, 0, hc)
-        f_dn.wait_recv()
-        s4 = pass_on(8, op_d, sib, hc, hc)
-        for s in (s0, s1, s2, s3, s4):
-            s.wait_recv()
-
-        kt = 512
-
-        if a == 0:
-            if c == 0:
-                gate[...] = jnp.zeros_like(gate)
-                up[...] = jnp.zeros_like(up)
-
-            def fwd(i, carry):
-                kk = pl.ds(al(c * cw + i * kt, kt), kt)
-                r = alls[0, :, kk]
-                gate[...] += dot_nt(r, wg[:, kk])
-                up[...] += dot_nt(r, wu[:, kk])
-                return carry
-
-            lax.fori_loop(0, cw // kt, fwd, 0)
-        else:
-            if c == 0:
-                back[...] = jnp.zeros_like(back)
-
-            def bwd(i, carry):
-                kk = pl.ds(al(c * cw + i * kt, kt), kt)
-                back[...] += dot_nt(alls[1, :, kk], wd[:, kk])
-                return carry
-
-            lax.fori_loop(0, cw // kt, bwd, 0)
+            col = (q % CH) * cw + b * sw
+            alls[q // CH, mine, col : col + sw] = dot(rhot, recvb[q]).astype(BF)
+        pass_on(q, 0, dp, up_d)
+        pass_on(q, 1, dp, dn_d)
+        pass_on(q, 2, dp, sib)
+        if q + DEPTH < 2 * CH:
+            dispatch(q + DEPTH)
+
+    def forward(q):
+        hops[q, 0].wait_recv()
+        pass_on(q, 3, dn_d, up_d, 0, hc)
+        pass_on(q, 4, dn_d, sib)
+        hops[q, 1].wait_recv()
+        pass_on(q, 5, up_d, dn_d, hc, hc)
+        pass_on(q, 6, up_d, sib)
+
+    def complete(q):
+        hops[q, 3].wait_recv()
+        pass_on(q, 7, op_d, sib, 0, hc)
+        hops[q, 5].wait_recv()
+        pass_on(q, 8, op_d, sib, hc, hc)
+        for j in (2, 4, 6, 7, 8):
+            hops[q, j].wait_recv()
+
+    def products(q):
+        c = q % CH
+
+        def fwd(i, carry):
+            kk = pl.ds(al(c * cw + i * kt, kt), kt)
+            r = alls[0, :, kk]
+            gate[...] += dot_nt(r, wg[:, kk])
+            up[...] += dot_nt(r, wu[:, kk])
+            return carry
+
+        def bwd(i, carry):
+            kk = pl.ds(al(c * cw + i * kt, kt), kt)
+            back[...] += dot_nt(alls[1, :, kk], wd[:, kk])
+            return carry
+
+        lax.fori_loop(0, cw // kt, fwd if q < CH else bwd, 0)
+
+    def activate(i, carry):
+        r = pl.ds(al(i * 128, 128), 128)
+        g, u = gate[r, :], up[r, :]
+        s = jax.nn.sigmoid(g)
+        act = g * s
+        hid[r, :] = (act * u).astype(BF)
+        gate[r, :] = u * s * (1.0 + g * (1.0 - s))
+        up[r, :] = act
+        return carry
+
+    for acc in (gate, up, back):
+        acc[...] = jnp.zeros_like(acc)
+    for q in range(2 * CH):
+        arrive(q)
+        if q > 0:
+            complete(q - 1)
+            products(q - 1)
+        forward(q)
+        if q == CH:
+            lax.fori_loop(0, 4, activate, 0)
+    complete(2 * CH - 1)
+    products(2 * CH - 1)
 
     pltpu.make_async_copy(gv_part, gv_part, small_r.at[0]).wait()
 
     def pointwise(i, carry):
         r = pl.ds(al(i * 128, 128), 128)
-        g, u, bk = gate[r, :], up[r, :], back[r, :]
-        gv = gv_all[r, 0:1]
-        s = jax.nn.sigmoid(g)
-        act = g * s
-        hidden = (act * u).astype(BF).astype(F32)
-        sc_p[r, :] = jnp.broadcast_to(jnp.sum(hidden * bk, axis=-1, keepdims=True), (128, 128))
-        dh = gv * bk
-        dgate = (dh * u * s * (1.0 + g * (1.0 - s))).astype(BF)
-        dup = (dh * act).astype(BF)
-        dgu[0, r, :] = dgate
-        dgu[1, r, :] = dup
-        tr[0, :, r] = hidden.T.astype(BF)
-        tr[1, :, r] = dgate.astype(F32).T.astype(BF)
-        tr[2, :, r] = dup.astype(F32).T.astype(BF)
+        dh = gv_all[r, 0:1] * back[r, :]
+        dgu[0, r, :] = (dh * gate[r, :]).astype(BF)
+        dgu[1, r, :] = (dh * up[r, :]).astype(BF)
         return carry
 
     lax.fori_loop(0, 4, pointwise, 0)
     dx = push(dgu, dgs, sib_s.at[2], sib_r.at[2], sib)
-
-    def send_score(d, carry):
-        to = lax.rem(dp + d, 8)
-        copy(
-            sc_p.at[pl.ds(al(to * cap, cap), cap)], sc_r.at[lax.rem(8 - d, 8)],
-            small_s.at[1], small_r.at[1], to,
-        ).start()
-        return carry
-
-    lax.fori_loop(1, 8, send_score, 0)
-    sc_part = sc_r.at[pl.ds(1, 7)]
-    pending.append(pltpu.make_async_copy(sc_part, sc_part, small_s.at[1]).wait)
-    ws0.wait_recv()
-    ws1.wait_recv()
-    dx.wait_recv()
 
     two = 2 * cap
     fw = half // RC
     hw = fw // 2
 
-    def part(yy, c):
+    def part(yy, c, ready=()):
         r = pl.ds(al(yy * two, two), two)
         w_at = pl.ds(al(k * half + c * fw, fw), fw)
         o_at = pl.ds(c * fw, fw)
         t = dot(dgu[0, r, :], wg[:, w_at])
         t += dot(dgu[1, r, :], wu[:, w_at])
+        for d in ready:
+            d.wait_recv()
         t += dot(dgs[0, r, :], wsib[0, :, o_at])
         t += dot(dgs[1, r, :], wsib[1, :, o_at])
         return t
 
-    a_cp, b_cp, x_cp = [], [], []
-    for c in range(RC):
-        t = part(y_op, c)
+    a_cp, b_cp, x_cp = {}, {}, {}
+
+    def far_terms(c):
+        t = part(y_op, c, (ws0, ws1, dx) if c == 0 else ())
         a_s[c, 0] = t[:, :hw].astype(BF)
         a_s[c, 1] = t[:, hw:].astype(BF)
         for j, to in ((0, up_d), (1, dn_d)):
-            a_cp.append(push(a_s.at[c, j], a_r.at[c, j], rs_s.at[c, j], rs_r.at[c, j], to))
-    for c in range(RC):
+            a_cp[c, j] = push(a_s.at[c, j], a_r.at[c, j], rs_s.at[c, j], rs_r.at[c, j], to)
+
+    def near_terms(c):
         for j, (yy, to) in enumerate(((y_up, up_d), (y_dn, dn_d))):
             t = part(yy, c)
-            a_cp[2 * c + j].wait_recv()
+            a_cp[c, j].wait_recv()
             at = slice(0, hw) if j == 0 else slice(hw, fw)
             rest = slice(hw, fw) if j == 0 else slice(0, hw)
             b_s[c, j, :, at] = (t[:, at] + a_r[c, j].astype(F32)).astype(BF)
             b_s[c, j, :, rest] = t[:, rest].astype(BF)
-            b_cp.append(
-                push(b_s.at[c, j], b_r.at[c, j], rs_s.at[c, 2 + j], rs_r.at[c, 2 + j], to)
-            )
-    for c in range(RC):
+            b_cp[c, j] = push(b_s.at[c, j], b_r.at[c, j], rs_s.at[c, 2 + j], rs_r.at[c, 2 + j], to)
+
+    def own_sum(c):
         t = part(y, c)
-        b_cp[2 * c].wait_recv()
-        b_cp[2 * c + 1].wait_recv()
+        b_cp[c, 0].wait_recv()
+        b_cp[c, 1].wait_recv()
         t += b_r[c, 0].astype(F32) + b_r[c, 1].astype(F32)
         dg_own[c] = t.astype(BF)
-        x_cp.append(
-            push(
-                dg_own.at[c, pl.ds(al((1 - k) * cap, cap), cap)], dg_x.at[c],
-                rs_s.at[c, 4], rs_r.at[c, 4], sib,
-            )
-        )
+        theirs = dg_own.at[c, pl.ds(al((1 - k) * cap, cap), cap)]
+        x_cp[c] = push(theirs, dg_x.at[c], rs_s.at[c, 4], rs_r.at[c, 4], sib)
 
     row_i = lax.broadcasted_iota(jnp.int32, (nrow, cap), 0).astype(F32)
-    for c in range(RC):
+
+    def give_back(c):
         x_cp[c].wait_recv()
         mine_half = dg_own[c, pl.ds(al(k * cap, cap), cap), :]
         theirs = dg_x[c]
-        first = k == 0
-        h0 = jnp.where(first, mine_half, theirs)
-        h1 = jnp.where(first, theirs, mine_half)
+        h0 = jnp.where(k == 0, mine_half, theirs)
+        h1 = jnp.where(k == 0, theirs, mine_half)
         acc = jnp.zeros((nrow, hw), F32)
         for b in range(SUB):
             hot = jnp.where(rfl_r + b * SLOTS == row_i, 1.0, 0.0).astype(BF)
@@ -321,6 +322,45 @@
         ret_s[c] = acc.astype(BF)
         ret_r[c, own, :] = ret_s[c, own, :]
         spread(ret_s.at[c], ret_r.at[c], r_send.at[c], r_recv.at[c])
+
+    far_terms(0)
+    far_terms(1)
+    near_terms(0)
+    far_terms(2)
+    near_terms(1)
+    own_sum(0)
+    for c in range(RC):
+        if c + 3 < RC:
+            far_terms(c + 3)
+        if c + 2 < RC:
+            near_terms(c + 2)
+        if c + 1 < RC:
+            own_sum(c + 1)
+        give_back(c)
+
+    def turn(i, carry):
+        r = pl.ds(al(i * 128, 128), 128)
+        hidden = hid[r, :].astype(F32)
+        total = jnp.sum(hidden * back[r, :], axis=-1, keepdims=True)
+        sc_p[r, :] = jnp.broadcast_to(total, (128, 128))
+        tr[0, :, r] = hidden.T.astype(BF)
+        tr[1, :, r] = dgu[0, r, :].astype(F32).T.astype(BF)
+        tr[2, :, r] = dgu[1, r, :].astype(F32).T.astype(BF)
+        return carry
+
+    lax.fori_loop(0, 4, turn, 0)
+
+    def send_score(d, carry):
+        to = lax.rem(dp + d, 8)
+        copy(
+            sc_p.at[pl.ds(al(to * cap, cap), cap)], sc_r.at[lax.rem(8 - d, 8)],
+            small_s.at[1], small_r.at[1], to,
+        ).start()
+        return carry
+
+    lax.fori_loop(1, 8, send_score, 0)
+    sc_part = sc_r.at[pl.ds(1, 7)]
+    pending.append(pltpu.make_async_copy(sc_part, sc_part, small_s.at[1]).wait)
 
     nt = 512
 
@@ -361,6 +401,29 @@
         wait()
     for c in stores:
         c.wait()
+
+
+def hand_over(*refs):
+    n = (len(refs) - 2) // 3
+    came, left = refs[-2], refs[-1]
+    moves = []
+    for i in range(n):
+        src, dst, mid = refs[i], refs[n + i], refs[2 * n + i]
+        rows = src.shape[-2]
+        step = PIECE if rows % PIECE == 0 else rows
+        for j in range(rows // step):
+            at = (0,) * (len(src.shape) - 2) + (pl.ds(j * step, step),)
+            moves.append((
+                pltpu.make_async_copy(src.at[at], mid.at[at], came.at[i, j]),
+                pltpu.make_async_copy(mid.at[at], dst.at[at], left.at[i, j]),
+            ))
+    for first, _ in moves:
+        first.start()
+    for first, second in moves:
+        first.wait()
+        second.start()
+    for _, second in moves:
+        second.wait()
 
 
 def on_device(tokens, cotangent, picks, gate_values, w_gate, w_up, w_down):
@@ -377,7 +440,7 @@
     vm = pl.BlockSpec(memory_space=pltpu.VMEM)
     hbm = pl.BlockSpec(memory_space=pl.ANY)
     dma = pltpu.SemaphoreType.DMA
-    d_tokens, score, dwg, dwu, dwd = pl.pallas_call(
+    results = pl.pallas_call(
         functools.partial(kernel, experts),
         out_shape=(
             jax.ShapeDtypeStruct((tok_rows, width), BF),
@@ -401,6 +464,7 @@
             pltpu.VMEM((rows, ff), F32),
             pltpu.VMEM((rows, ff), F32),
             pltpu.VMEM((rows, ff), F32),
+            pltpu.VMEM((rows, ff), BF),
             pltpu.VMEM((2, rows, ff), BF),
             pltpu.VMEM((2, rows, ff), BF),
             pltpu.VMEM((3, ff, rows), BF),
@@ -435,6 +499,13 @@
         tokens, cotangent, picks, gate_values,
         jnp.swapaxes(w_gate, 1, 2), jnp.swapaxes(w_up, 1, 2), w_down,
     )
+    d_tokens, score, dwg, dwu, dwd = pl.pallas_call(
+        hand_over,
+        out_shape=[jax.ShapeDtypeStruct(r.shape, r.dtype) for r in results],
+        in_specs=[hbm] * 5,
+        out_specs=[hbm] * 5,
+        scratch_shapes=[pltpu.VMEM(r.shape, r.dtype) for r in results] + [dma((5, 4)), dma((5, 4))],
+    )(*results)
     return d_tokens, score, jnp.swapaxes(dwg, 1, 2), jnp.swapaxes(dwu, 1, 2), dwd
 
 

time: 152 us -> 123 us (0.81)
  Pallas kernels: 143 us -> 122 us
  local copies, waits for them, and re-layouts: 8.02 us -> 0 us
    pallas_call x1, Pallas kernels: 143 us -> 116 us  [on_device(): pl.pallas_call(functools.partial(kernel, experts), out_shape=(jax.ShapeDt...]
    unnamed x13 -> x0, local copies, waits for them, and re-layouts: 8.02 us -> none
    pallas_call x0 -> x1, Pallas kernels: none -> 5.33 us  [on_device(): pl.pallas_call(hand_over, out_shape=[jax.ShapeDtypeStruct(r.shape, r.dtyp...]
where the time goes in v3:
time: 123 us; the launch traced here: 122 us
  Pallas kernels  122 us (99%)
    pallas_call x1, Pallas kernels, on_device(): pl.pallas_call(functools.partial(kernel, experts), out_shape=(jax.ShapeDt...  116 us
    pallas_call x1, Pallas kernels, on_device(): pl.pallas_call(hand_over, out_shape=[jax.ShapeDtypeStruct(r.shape, r.dtyp...  5.33 us

profile of v3, /device:TPU:1, one launch (start us, length us, event | category | flops | bytes accessed | tf_op | source)
XLA Modules:
  0.0 122.4 jit_solution(14480409567591965204)
XLA Ops:
  0.6 116.5 %shard_map.110 = (bf16[128,4096]{1,0:T(8,128)(2,1)}, f32[1,1,64]{2,1,0:T(1,128)}, bf16[1,192,4096]{2,1,0:T(8,128)(2,1)}, bf16[1,192,4096]{2,1,0:T(8,128)(2,1)}, bf16[1,192,4096]{2,1,0:T(8,128)(2,1)}) custom-call(bf16[128,4096]{1,0:T(8,128)(2,1)} %tok.1, bf16[128,4096]{1,0:T(8,128)(2,1)} %cot.1, s32[1,32,64]{2,1,0:T(8,128)} %picks.1, ...), custom_call_target="tpu_custom_call" | custom-call | flops 6442450944 | bytes 12582912 | tf_op jit(solution)/shard_map/pallas_call | solution.py:443
  117.1 5.3 %shard_map.111 = (bf16[128,4096]{1,0:T(8,128)(2,1)}, f32[1,1,64]{2,1,0:T(1,128)}, bf16[1,192,4096]{2,1,0:T(8,128)(2,1)}, bf16[1,192,4096]{2,1,0:T(8,128)(2,1)}, bf16[1,192,4096]{2,1,0:T(8,128)(2,1)}) custom-call(bf16[128,4096]{1,0:T(8,128)(2,1)} %get-tuple-element.15.refs_0_, f32[1,1,64]{2,1,0:T(1,128)} %get-tuple-element.16.refs_1_, ...), custom_call_target="tpu_custom_call" | custom-call | tf_op jit(solution)/shard_map/pallas_call | solution.py:502

commit v4 on v3

--- a/solution.py
+++ b/solution.py
@@ -35,7 +35,7 @@
 def kernel(
     experts, tok, cot, picks, gates, wg_h, wu_h, wd_h,
     dtok, score, dwg_h, dwu_h, dwd_h,
-    sendb, recvb, alls, gvb, gv_all, wg, wu, wd, wsib, gate, up, back, hid, dgu, dgs, tr,
+    gcat, ccat, bcat, fcat, sendb, recvb, alls, gvb, gv_all, wg, wu, wd, wsib, gate, up, back, hid, dgu, dgs, tr,
     a_s, a_r, b_s, b_r, dg_own, dg_x, ret_s, ret_r, sc_p, sc_r, dwg, dwu, dwd,
     d_send, d_recv, g_send, g_recv, small_s, small_r, sib_s, sib_r, rs_s, rs_r, r_send, r_recv, loc,
 ):
@@ -126,7 +126,8 @@
     row_sub = lax.rem(lax.broadcasted_iota(jnp.int32, (nrow, tok_rows), 0) // SLOTS, SUB)
     col_tok = lax.broadcasted_iota(jnp.int32, (nrow, tok_rows), 1)
     match = sidx_c == col_tok.astype(F32)
-    hots = [jnp.where(match & (row_sub == b), 1.0, 0.0).astype(BF) for b in range(SUB)]
+    for b in range(SUB):
+        gcat[:, b * tok_rows : (b + 1) * tok_rows] = jnp.where(match & (row_sub == b), 1.0, 0.0).astype(BF)
     own = pl.ds(al(ex * ROWS, ROWS), ROWS)
 
     def dispatch(q):
@@ -135,10 +136,8 @@
     for q in range(2 * CH):
         src = tok if q < CH else cot
         base = (q % CH) * cw
-        acc = dot(hots[0], src[:, base : base + sw])
-        for b in range(1, SUB):
-            acc += dot(hots[b], src[:, base + b * sw : base + (b + 1) * sw])
-        sendb[q] = acc.astype(BF)
+        stacked = jnp.concatenate([src[:, base + b * sw : base + (b + 1) * sw] for b in range(SUB)], axis=0)
+        sendb[q] = dot(gcat[...], stacked).astype(BF)
         recvb[q, own, :] = sendb[q, own, :]
         if q == 0:
             pl.semaphore_wait(barrier, experts - 1 + 7)
@@ -151,7 +150,8 @@
     behind = lax.broadcasted_iota(jnp.int32, (cap, cap), 0) > lax.broadcasted_iota(jnp.int32, (cap, cap), 1)
     twins = jnp.where((src_col[:, :cap] == src_row[:cap]) & behind, 1.0, 0.0)
     rfl_c = src_col[:, 0:1] * ROWS + jnp.sum(twins, axis=-1, keepdims=True)
-    rfl_r = jnp.broadcast_to(rfl_c, (cap, 128)).T[0:1]
+    at_c = jnp.concatenate([rfl_c + b * SLOTS for b in range(SUB)], axis=0)
+    at_r = jnp.broadcast_to(at_c, (SUB * cap, 128)).T[0:1]
     sidx_r = jnp.broadcast_to(sidx_c, (nrow, 128)).T[0:1]
     gvb[...] = jnp.broadcast_to(gates[0].astype(F32), (128, cap)).T
 
@@ -171,7 +171,16 @@
     for c in loads:
         c.wait()
 
-    lane_row = lax.broadcasted_iota(jnp.int32, (cap, nrow), 1).astype(F32)
+    lane_row = lax.broadcasted_iota(jnp.int32, (SUB * cap, nrow), 1).astype(F32)
+    ccat[...] = jnp.where(at_c == lane_row, 1.0, 0.0).astype(BF)
+    row_i = lax.broadcasted_iota(jnp.int32, (nrow, SUB * cap), 0).astype(F32)
+    bcat[...] = jnp.where(at_r == row_i, 1.0, 0.0).astype(BF)
+    sub_r = lax.rem(lax.broadcasted_iota(jnp.int32, (tok_rows, nrow), 1) // SLOTS, SUB)
+    tok_i = lax.broadcasted_iota(jnp.int32, (tok_rows, nrow), 0).astype(F32)
+    tmatch = sidx_r == tok_i
+    for b in range(SUB):
+        fcat[b * tok_rows : (b + 1) * tok_rows, :] = jnp.where(tmatch & (sub_r == b), 1.0, 0.0).astype(BF)
+
     hc = cap // 2
     kt = 512
     hops = {}
@@ -184,10 +193,10 @@
 
     def arrive(q):
         await_bytes(recvb.at[q], d_recv.at[q])
+        packed = dot(ccat[...], recvb[q]).astype(BF)
         for b in range(SUB):
-            rhot = jnp.where(rfl_c + b * SLOTS == lane_row, 1.0, 0.0).astype(BF)
             col = (q % CH) * cw + b * sw
-            alls[q // CH, mine, col : col + sw] = dot(rhot, recvb[q]).astype(BF)
+            alls[q // CH, mine, col : col + sw] = packed[b * cap : (b + 1) * cap]
         pass_on(q, 0, dp, up_d)
         pass_on(q, 1, dp, dn_d)
         pass_on(q, 2, dp, sib)
@@ -306,20 +315,14 @@
         theirs = dg_own.at[c, pl.ds(al((1 - k) * cap, cap), cap)]
         x_cp[c] = push(theirs, dg_x.at[c], rs_s.at[c, 4], rs_r.at[c, 4], sib)
 
-    row_i = lax.broadcasted_iota(jnp.int32, (nrow, cap), 0).astype(F32)
-
     def give_back(c):
         x_cp[c].wait_recv()
         mine_half = dg_own[c, pl.ds(al(k * cap, cap), cap), :]
         theirs = dg_x[c]
         h0 = jnp.where(k == 0, mine_half, theirs)
         h1 = jnp.where(k == 0, theirs, mine_half)
-        acc = jnp.zeros((nrow, hw), F32)
-        for b in range(SUB):
-            hot = jnp.where(rfl_r + b * SLOTS == row_i, 1.0, 0.0).astype(BF)
-            src = h0 if b < 2 else h1
-            acc += dot(hot, src[:, (b % 2) * hw : (b % 2 + 1) * hw])
-        ret_s[c] = acc.astype(BF)
+        stacked = jnp.concatenate([h0[:, :hw], h0[:, hw:], h1[:, :hw], h1[:, hw:]], axis=0)
+        ret_s[c] = dot(bcat[...], stacked).astype(BF)
         ret_r[c, own, :] = ret_s[c, own, :]
         spread(ret_s.at[c], ret_r.at[c], r_send.at[c], r_recv.at[c])
 
@@ -387,15 +390,12 @@
         total += sc_r[j]
     score[0] = total.T[0:1]
 
-    sub_r = lax.rem(lax.broadcasted_iota(jnp.int32, (tok_rows, nrow), 1) // SLOTS, SUB)
-    tok_i = lax.broadcasted_iota(jnp.int32, (tok_rows, nrow), 0).astype(F32)
-    tmatch = sidx_r == tok_i
     for c in range(RC):
         await_bytes(ret_r.at[c], r_recv.at[c])
+        sums = dot(fcat[...], ret_r[c]).astype(BF)
         for b in range(SUB):
-            hot = jnp.where(tmatch & (sub_r == b), 1.0, 0.0).astype(BF)
             col = (b // 2) * half + c * fw + (b % 2) * hw
-            dtok[:, col : col + hw] = dot(hot, ret_r[c]).astype(BF)
+            dtok[:, col : col + hw] = sums[b * tok_rows : (b + 1) * tok_rows]
 
     for wait in pending:
         wait()
@@ -452,6 +452,10 @@
         in_specs=[vm] * 4 + [hbm] * 3,
         out_specs=[vm] * 2 + [hbm] * 3,
         scratch_shapes=[
+            pltpu.VMEM((nrow, SUB * tok_rows), BF),
+            pltpu.VMEM((SUB * cap, nrow), BF),
+            pltpu.VMEM((nrow, SUB * cap), BF),
+            pltpu.VMEM((SUB * tok_rows, nrow), BF),
             pltpu.VMEM((2 * CH, nrow, cw // SUB), BF),
             pltpu.VMEM((2 * CH, nrow, cw // SUB), BF),
             pltpu.VMEM((2, rows, width), BF),

time: 123 us -> 123 us (level)
  no operation moved by 1% of the time
where the time goes in v4:
time: 123 us; the launch traced here: 122 us
  Pallas kernels  121 us (98%)
    pallas_call x1, Pallas kernels, on_device(): pl.pallas_call(functools.partial(kernel, experts), out_shape=(jax.ShapeDt...  116 us
    pallas_call x1, Pallas kernels, on_device(): pl.pallas_call(hand_over, out_shape=[jax.ShapeDtypeStruct(r.shape, r.dtyp...  5.33 us

profile of v4, /device:TPU:1, one launch (start us, length us, event | category | flops | bytes accessed | tf_op | source)
XLA Modules:
  0.0 122.1 jit_solution(3474036148210243103)
XLA Ops:
  0.6 116.2 %shard_map.110 = (bf16[128,4096]{1,0:T(8,128)(2,1)}, f32[1,1,64]{2,1,0:T(1,128)}, bf16[1,192,4096]{2,1,0:T(8,128)(2,1)}, bf16[1,192,4096]{2,1,0:T(8,128)(2,1)}, bf16[1,192,4096]{2,1,0:T(8,128)(2,1)}) custom-call(bf16[128,4096]{1,0:T(8,128)(2,1)} %tok.1, bf16[128,4096]{1,0:T(8,128)(2,1)} %cot.1, s32[1,32,64]{2,1,0:T(8,128)} %picks.1, ...), custom_call_target="tpu_custom_call" | custom-call | flops 6442450944 | bytes 12582912 | tf_op jit(solution)/shard_map/pallas_call | solution.py:443
  116.8 5.3 %shard_map.111 = (bf16[128,4096]{1,0:T(8,128)(2,1)}, f32[1,1,64]{2,1,0:T(1,128)}, bf16[1,192,4096]{2,1,0:T(8,128)(2,1)}, bf16[1,192,4096]{2,1,0:T(8,128)(2,1)}, bf16[1,192,4096]{2,1,0:T(8,128)(2,1)}) custom-call(bf16[128,4096]{1,0:T(8,128)(2,1)} %get-tuple-element.15.refs_0_, f32[1,1,64]{2,1,0:T(1,128)} %get-tuple-element.16.refs_1_, ...), custom_call_target="tpu_custom_call" | custom-call | tf_op jit(solution)/shard_map/pallas_call | solution.py:506

commit v5 on v4

--- a/solution.py
+++ b/solution.py
@@ -404,26 +404,12 @@
 
 
 def hand_over(*refs):
-    n = (len(refs) - 2) // 3
-    came, left = refs[-2], refs[-1]
-    moves = []
-    for i in range(n):
-        src, dst, mid = refs[i], refs[n + i], refs[2 * n + i]
-        rows = src.shape[-2]
-        step = PIECE if rows % PIECE == 0 else rows
-        for j in range(rows // step):
-            at = (0,) * (len(src.shape) - 2) + (pl.ds(j * step, step),)
-            moves.append((
-                pltpu.make_async_copy(src.at[at], mid.at[at], came.at[i, j]),
-                pltpu.make_async_copy(mid.at[at], dst.at[at], left.at[i, j]),
-            ))
-    for first, _ in moves:
-        first.start()
-    for first, second in moves:
-        first.wait()
-        second.start()
-    for _, second in moves:
-        second.wait()
+    n = (len(refs) - 1) // 2
+    copies = [pltpu.make_async_copy(refs[i], refs[n + i], refs[-1].at[i]) for i in range(n)]
+    for c in copies:
+        c.start()
+    for c in copies:
+        c.wait()
 
 
 def on_device(tokens, cotangent, picks, gate_values, w_gate, w_up, w_down):
@@ -494,7 +480,7 @@
             dma((3,)),
         ],
         compiler_params=pltpu.CompilerParams(
-            collective_id=0, has_side_effects=True, vmem_limit_bytes=58 * 2**20
+            collective_id=0, has_side_effects=True, vmem_limit_bytes=46 * 2**20
         ),
         cost_estimate=pl.CostEstimate(
             flops=2 * 8 * rows * width * ff, bytes_accessed=12 * 2**20, transcendentals=rows * ff
@@ -506,9 +492,10 @@
     d_tokens, score, dwg, dwu, dwd = pl.pallas_call(
         hand_over,
         out_shape=[jax.ShapeDtypeStruct(r.shape, r.dtype) for r in results],
-        in_specs=[hbm] * 5,
+        in_specs=[vm] * 5,
         out_specs=[hbm] * 5,
-        scratch_shapes=[pltpu.VMEM(r.shape, r.dtype) for r in results] + [dma((5, 4)), dma((5, 4))],
+        scratch_shapes=[dma((5,))],
+        compiler_params=pltpu.CompilerParams(vmem_limit_bytes=16 * 2**20),
     )(*results)
     return d_tokens, score, jnp.swapaxes(dwg, 1, 2), jnp.swapaxes(dwu, 1, 2), dwd
 

time: 123 us -> 121 us (0.984)
  Pallas kernels: 121 us -> 116 us
  local copies, waits for them, and re-layouts: 0 us -> 3.81 us
    unnamed x0 -> x8, local copies, waits for them, and re-layouts: none -> 3.81 us
    pallas_call x1, Pallas kernels: 116 us -> 113 us  [on_device(): pl.pallas_call(functools.partial(kernel, experts), out_shape=(jax.ShapeDt...]
    pallas_call x1, Pallas kernels: 5.33 us -> 2.57 us  [on_device(): pl.pallas_call(hand_over, out_shape=[jax.ShapeDtypeStruct(r.shape, r.dtyp...]
where the time goes in v5:
time: 121 us; the launch traced here: 120 us
  Pallas kernels  116 us (96%)
  local copies, waits for them, and re-layouts  3.81 us (3%)
    pallas_call x1, Pallas kernels, on_device(): pl.pallas_call(functools.partial(kernel, experts), out_shape=(jax.ShapeDt...  113 us
    unnamed x8, local copies, waits for them, and re-layouts  3.81 us
    pallas_call x1, Pallas kernels, on_device(): pl.pallas_call(hand_over, out_shape=[jax.ShapeDtypeStruct(r.shape, r.dtyp...  2.57 us

profile of v5, /device:TPU:1, one launch (start us, length us, event | category | flops | bytes accessed | tf_op | source)
XLA Modules:
  0.0 120.2 jit_solution(8763830603441268952)
XLA Ops:
  0.6 0.0 copy-start
  0.6 1.2 %copy-done = bf16[128,4096]{1,0:T(8,128)(2,1)S(1)} copy-done((bf16[128,4096]{1,0:T(8,128)(2,1)S(1)}, bf16[128,4096]{1,0:T(8,128)(2,1)}, u32[]{:S(2)}) %copy-start) | copy-done | bytes 1048600
  1.9 0.0 copy-start.1
  1.9 1.2 %copy-done.1 = bf16[128,4096]{1,0:T(8,128)(2,1)S(1)} copy-done((bf16[128,4096]{1,0:T(8,128)(2,1)S(1)}, bf16[128,4096]{1,0:T(8,128)(2,1)}, u32[]{:S(2)}) %copy-start.1) | copy-done | bytes 1048600
  3.1 0.0 copy-start.2
  3.1 0.7 copy-done.2
  3.8 0.0 copy-start.3
  3.8 0.7 copy-done.3
  4.5 113.2 %shard_map.110 = (bf16[128,4096]{1,0:T(8,128)(2,1)S(1)}, f32[1,1,64]{2,1,0:T(1,128)S(1)}, bf16[1,192,4096]{2,1,0:T(8,128)(2,1)S(1)}, bf16[1,192,4096]{2,1,0:T(8,128)(2,1)S(1)}, bf16[1,192,4096]{2,1,0:T(8,128)(2,1)S(1)}) custom-call(bf16[128,4096]{1,0:T(8,128)(2,1)S(1)} %copy-done, bf16[128,4096]{1,0:T(8,128)(2,1)S(1)} %copy-done.1, ...), custom_call_target="tpu_custom_call" | custom-call | flops 6442450944 | bytes 12582912 | tf_op jit(solution)/shard_map/pallas_call | solution.py:429
  117.6 2.6 %shard_map.111 = (bf16[128,4096]{1,0:T(8,128)(2,1)}, f32[1,1,64]{2,1,0:T(1,128)}, bf16[1,192,4096]{2,1,0:T(8,128)(2,1)}, bf16[1,192,4096]{2,1,0:T(8,128)(2,1)}, bf16[1,192,4096]{2,1,0:T(8,128)(2,1)}) custom-call(bf16[128,4096]{1,0:T(8,128)(2,1)S(1)} %get-tuple-element.15.refs_0_, f32[1,1,64]{2,1,0:T(1,128)S(1)} %get-tuple-element.16.refs_1_, ...), custom_call_target="tpu_custom_call" | custom-call | tf_op jit(solution)/shard_map/pallas_call | solution.py:492
Async XLA Ops:
  0.6 1.2 %copy-start = (bf16[128,4096]{1,0:T(8,128)(2,1)S(1)}, bf16[128,4096]{1,0:T(8,128)(2,1)}, u32[]{:S(2)}) copy-start(bf16[128,4096]{1,0:T(8,128)(2,1)} %tok.1) | copy-start | bytes 3145732
  1.9 1.2 %copy-start.1 = (bf16[128,4096]{1,0:T(8,128)(2,1)S(1)}, bf16[128,4096]{1,0:T(8,128)(2,1)}, u32[]{:S(2)}) copy-start(bf16[128,4096]{1,0:T(8,128)(2,1)} %cot.1) | copy-start | bytes 3145732
  3.1 0.7 copy-start.2
  3.8 0.7 copy-start.3

commit v6 on v5

--- a/solution.py
+++ b/solution.py
@@ -17,7 +17,7 @@
 CH = 2
 RC = 4
 PIECE = 64
-DEPTH = 2
+DEPTH = 4
 
 
 def dot(a, b):

time: 121 us -> 121 us (level)
  no operation moved by 1% of the time
where the time goes in v6:
time: 121 us; the launch traced here: 120 us
  Pallas kernels  116 us (96%)
  local copies, waits for them, and re-layouts  3.81 us (3%)
    pallas_call x1, Pallas kernels, on_device(): pl.pallas_call(functools.partial(kernel, experts), out_shape=(jax.ShapeDt...  113 us
    unnamed x8, local copies, waits for them, and re-layouts  3.81 us
    pallas_call x1, Pallas kernels, on_device(): pl.pallas_call(hand_over, out_shape=[jax.ShapeDtypeStruct(r.shape, r.dtyp...  2.57 us

profile of v6, /device:TPU:1, one launch (start us, length us, event | category | flops | bytes accessed | tf_op | source)
XLA Modules:
  0.0 120.2 jit_solution(421665122704792048)
XLA Ops:
  0.6 0.0 copy-start
  0.6 1.2 %copy-done = bf16[128,4096]{1,0:T(8,128)(2,1)S(1)} copy-done((bf16[128,4096]{1,0:T(8,128)(2,1)S(1)}, bf16[128,4096]{1,0:T(8,128)(2,1)}, u32[]{:S(2)}) %copy-start) | copy-done | bytes 1048600
  1.9 0.0 copy-start.1
  1.9 1.2 %copy-done.1 = bf16[128,4096]{1,0:T(8,128)(2,1)S(1)} copy-done((bf16[128,4096]{1,0:T(8,128)(2,1)S(1)}, bf16[128,4096]{1,0:T(8,128)(2,1)}, u32[]{:S(2)}) %copy-start.1) | copy-done | bytes 1048600
  3.1 0.0 copy-start.2
  3.1 0.7 copy-done.2
  3.8 0.0 copy-start.3
  3.8 0.7 copy-done.3
  4.5 113.2 %shard_map.110 = (bf16[128,4096]{1,0:T(8,128)(2,1)S(1)}, f32[1,1,64]{2,1,0:T(1,128)S(1)}, bf16[1,192,4096]{2,1,0:T(8,128)(2,1)S(1)}, bf16[1,192,4096]{2,1,0:T(8,128)(2,1)S(1)}, bf16[1,192,4096]{2,1,0:T(8,128)(2,1)S(1)}) custom-call(bf16[128,4096]{1,0:T(8,128)(2,1)S(1)} %copy-done, bf16[128,4096]{1,0:T(8,128)(2,1)S(1)} %copy-done.1, ...), custom_call_target="tpu_custom_call" | custom-call | flops 6442450944 | bytes 12582912 | tf_op jit(solution)/shard_map/pallas_call | solution.py:429
  117.6 2.6 %shard_map.111 = (bf16[128,4096]{1,0:T(8,128)(2,1)}, f32[1,1,64]{2,1,0:T(1,128)}, bf16[1,192,4096]{2,1,0:T(8,128)(2,1)}, bf16[1,192,4096]{2,1,0:T(8,128)(2,1)}, bf16[1,192,4096]{2,1,0:T(8,128)(2,1)}) custom-call(bf16[128,4096]{1,0:T(8,128)(2,1)S(1)} %get-tuple-element.15.refs_0_, f32[1,1,64]{2,1,0:T(1,128)S(1)} %get-tuple-element.16.refs_1_, ...), custom_call_target="tpu_custom_call" | custom-call | tf_op jit(solution)/shard_map/pallas_call | solution.py:492
Async XLA Ops:
  0.6 1.2 %copy-start = (bf16[128,4096]{1,0:T(8,128)(2,1)S(1)}, bf16[128,4096]{1,0:T(8,128)(2,1)}, u32[]{:S(2)}) copy-start(bf16[128,4096]{1,0:T(8,128)(2,1)} %tok.1) | copy-start | bytes 3145732
  1.9 1.2 %copy-start.1 = (bf16[128,4096]{1,0:T(8,128)(2,1)S(1)}, bf16[128,4096]{1,0:T(8,128)(2,1)}, u32[]{:S(2)}) copy-start(bf16[128,4096]{1,0:T(8,128)(2,1)} %cot.1) | copy-start | bytes 3145732
  3.1 0.7 copy-start.2
  3.8 0.7 copy-start.3
